TPU v7x, 32 devices: a whole 2x2x4 slice. The times are simulated.
32 devices in a mesh: tm: 8 (over z, x), row: 2 (over y), col: 2 (over core).
Axes of the slice: x: 2, y: 2, z: 4, core: 2. Of those that a mesh axis runs over, the one named last changes fastest.
Arguments:
- features: bfloat16 [16, 12, 32, 512], P('tm', 'row', 'col'), may hold values from -16 to 16, as said below
- gn1_gain: float32 [512], replicated, may hold values from 0.1 to 1.9
- gn1_bias: float32 [512], replicated, may hold values from -3 to 3
- conv1_weight: bfloat16 [27, 512, 256], P(None, ('row', 'col')), may hold values from -0.0546875 to 0.0546875
- conv1_bias: float32 [256], replicated, may hold values from -3 to 3
- skip_weight: bfloat16 [1, 512, 256], P(None, ('row', 'col')), may hold values from -0.25 to 0.25
- gn2_gain: float32 [256], replicated, may hold values from 0.1 to 1.9
- gn2_bias: float32 [256], replicated, may hold values from -3 to 3
- conv2_weight: bfloat16 [27, 256, 256], P(None, ('row', 'col')), may hold values from -0.078125 to 0.078125
- conv2_bias: float32 [256], replicated, may hold values from -3 to 3
Outputs:
- block_out: bfloat16 [16, 12, 32, 256], P('tm', 'row', 'col')
Inputs may be any that keep to these rules, and one draw needn't show every extreme that they name: Latent features of the decoder, of mixed scales over frames, positions and channels.
All inputs are finite; a program needn't handle non-finite values.
Results may differ from a plain program's by a relative error of at most 0.0065.
Values may be sent and summed in bfloat16 or wider, within the bound.
A program may use at most 64 MiB of HBM per device.

v0:
```python
import jax
import jax.numpy as jnp
from jax import lax
from jax.sharding import PartitionSpec as P

GROUPS = 32


def passed_along(block, axis, distance):
    devices = range(lax.axis_size(axis))
    route = [(i - distance, i) for i in devices if i - distance in devices]
    return lax.ppermute(block, axis, route)


def with_halo(array, sides, width):
    for axis, dim in sides:
        size, length = (lax.axis_size(axis), array.shape[dim])
        up = [(i, (i + 1) % size) for i in range(size - 1)]
        down = [(j, i) for i, j in up]
        last = lax.slice_in_dim(array, length - width, length, axis=dim)
        leading = lax.slice_in_dim(array, 0, width, axis=dim)
        before = lax.ppermute(last, axis, up)
        after = lax.ppermute(leading, axis, down)
        array = jnp.concatenate([before, array, after], axis=dim)
    return array


def group_silu(values, gain, shift, groups, total_rows):
    chans = values.shape[-1]
    per_group = chans // groups
    grouped = values.reshape(-1, groups, per_group)
    count = float(total_rows * per_group)
    mean = lax.psum(jnp.sum(grouped, axis=(0, 2)), ("tm", "row", "col")) / count
    centred = grouped - mean[None, :, None]
    spread = lax.psum(jnp.sum(centred * centred, axis=(0, 2)), ("tm", "row", "col")) / count
    normed = (grouped - mean[None, :, None]) * lax.rsqrt(spread + 1e-06)[None, :, None]
    normed = normed.reshape(values.shape) * gain + shift
    return jax.nn.silu(normed).astype(jnp.bfloat16)


def conv_taps(padded, weight, frames, rows, cols):
    chans = padded.shape[3]
    total = jnp.zeros((frames * rows * cols, weight.shape[2]), jnp.float32)
    for dt in range(3):
        pieces = []
        for tap in range(9):
            dy, dx = (tap // 3, tap % 3)
            pieces.append(
                padded[dt : dt + frames, dy : dy + rows, dx : dx + cols].reshape(-1, chans)
            )
        stacked = jnp.concatenate(pieces, axis=1)
        flat_weight = weight[9 * dt : 9 * dt + 9].reshape(9 * chans, weight.shape[2])
        total = total + jnp.dot(stacked, flat_weight, preferred_element_type=jnp.float32)
    return total


def time_edge(earlier, volume):
    first_twice = jnp.concatenate([volume[:1], volume[:1]], axis=0)
    earlier = jnp.where(lax.axis_index("tm") == 0, first_twice, earlier)
    return jnp.concatenate([earlier, volume], axis=0)


def edge_rows(padded):
    place = lax.axis_index("row")
    last = lax.axis_size("row") - 1
    top = jnp.where(place == 0, padded[:, 1:2], padded[:, 0:1])
    bottom = jnp.where(place == last, padded[:, -2:-1], padded[:, -1:])
    return jnp.concatenate([top, padded[:, 1:-1], bottom], axis=1)


def edge_cols(padded):
    place = lax.axis_index("col")
    last = lax.axis_size("col") - 1
    left = jnp.where(place == 0, padded[:, :, 1:2], padded[:, :, 0:1])
    right = jnp.where(place == last, padded[:, :, -2:-1], padded[:, :, -1:])
    return jnp.concatenate([left, padded[:, :, 1:-1], right], axis=2)


def per_device(
    features,
    gn1_gain,
    gn1_bias,
    conv1_weight,
    conv1_bias,
    skip_weight,
    gn2_gain,
    gn2_bias,
    conv2_weight,
    conv2_bias,
):
    frames, rows, cols, chans_in = features.shape
    chans_out = conv1_weight.shape[2]
    groups = GROUPS
    nrow = lax.axis_size("row")
    ncol = lax.axis_size("col")
    total_rows = lax.axis_size("tm") * nrow * ncol * frames * rows * cols
    flat_features = features.reshape(-1, chans_in)
    hidden1 = group_silu(features.astype(jnp.float32), gn1_gain, gn1_bias, groups, total_rows)
    earlier = passed_along(hidden1, "tm", 1)
    extended = time_edge(earlier, hidden1)
    padded = with_halo(extended, (("row", 1), ("col", 2)), 1)
    padded = edge_cols(edge_rows(padded))
    window = padded
    first = conv_taps(
        window, lax.all_gather(conv1_weight, ("row", "col"), axis=1, tiled=True), frames, rows, cols
    )
    second = jnp.dot(
        flat_features,
        lax.all_gather(skip_weight, ("row", "col"), axis=1, tiled=True)[0],
        preferred_element_type=jnp.float32,
    )
    middle = (first + conv1_bias).reshape(frames, rows, cols, chans_out)
    hidden2 = group_silu(middle, gn2_gain, gn2_bias, groups, total_rows)
    earlier_mid = passed_along(hidden2, "tm", 1)
    extended_mid = time_edge(earlier_mid, hidden2)
    padded_mid = with_halo(extended_mid, (("row", 1), ("col", 2)), 1)
    padded_mid = edge_cols(edge_rows(padded_mid))
    window = padded_mid
    conv_second = conv_taps(
        window, lax.all_gather(conv2_weight, ("row", "col"), axis=1, tiled=True), frames, rows, cols
    )
    block_out = (second + conv_second + conv2_bias).astype(jnp.bfloat16)
    return block_out.reshape(frames, rows, cols, chans_out)


def solution(mesh):
    in_specs = (
        P("tm", "row", "col", None),
        P(),
        P(),
        P(None, ("row", "col"), None),
        P(),
        P(None, ("row", "col"), None),
        P(),
        P(),
        P(None, ("row", "col"), None),
        P(),
    )
    out_specs = P("tm", "row", "col", None)
    return jax.shard_map(
        per_device, mesh=mesh, in_specs=in_specs, out_specs=out_specs, check_vma=False
    )
```

profile of v0, /device:TPU:0, one launch (start us, length us, event | category | flops | bytes accessed | tf_op | source)
XLA Modules:
  0.0 240.9 jit_solution(15294146134485765704)
XLA Ops:
  6.5 0.7 all-gather.3.cloned.1.call-update
  7.3 0.2 copy-done.4
  7.7 42.4 %psum.28 = f32[32]{0:T(128)S(1)} all-reduce(f32[32]{0:T(128)S(1)} %reduce_sum.51), channel_id=1, replica_groups=mesh['tm'=8,'row'=2,'col'=2] {'tm','row','col'}, use_global_device_ids=true, to_apply=%region_2.0 | all-reduce | flops 32 | bytes 256 | tf_op jit(solution)/shard_map/psum | solution.py:33
  50.5 40.4 %psum.29 = f32[32]{0:T(128)S(1)} all-reduce(f32[32]{0:T(128)S(1)} %reduce_sum.54), channel_id=1, replica_groups=mesh['tm'=8,'row'=2,'col'=2] {'tm','row','col'}, use_global_device_ids=true, to_apply=%region_5.6 | all-reduce | flops 32 | bytes 256 | tf_op jit(solution)/shard_map/psum | solution.py:35
  91.1 0.1 fusion.13
  91.3 4.2 %collective-permute-start = (bf16[2,6,16,512]{3,2,1,0:T(8,128)(2,1)S(1)}, bf16[2,6,16,512]{3,2,1,0:T(8,128)(2,1)S(1)}, u32[]{:S(2)}, u32[]{:S(2)}) collective-permute-start(bf16[2,6,16,512]{3,2,1,0:T(8,128)(2,1)S(1)} %fusion.13), channel_id=1, source_target_pairs={{0,4},{4,8},{8,12},{12,16},{16,20},{20,24},{24,28},{1,5},{5,9},{9,... | collective-permute-start | bytes 589832 | tf_op jit(solution)/shard_map/ppermute | solution.py:12
  95.5 3.2 %collective-permute-done = bf16[2,6,16,512]{3,2,1,0:T(8,128)(2,1)S(1)} collective-permute-done((bf16[2,6,16,512]{3,2,1,0:T(8,128)(2,1)S(1)}, bf16[2,6,16,512]{3,2,1,0:T(8,128)(2,1)S(1)}, u32[]{:S(2)}, u32[]{:S(2)}) %collective-permute-start) | collective-permute-done | bytes 196640 | tf_op jit(solution)/shard_map/ppermute | solution.py:12
  98.7 3.2 %collective-permute-start.1 = (bf16[4,1,16,512]{3,2,1,0:T(8,128)(2,1)S(1)}, bf16[4,1,16,512]{3,2,1,0:T(8,128)(2,1)S(1)}, u32[]{:S(2)}, u32[]{:S(2)}) collective-permute-start(bf16[4,1,16,512]{3,2,1,0:T(8,128)(2,1)S(1)} %get-tuple-element.44), channel_id=1, source_target_pairs={{0,2},{1,3},{4,6},{5,7},{8,10},{9,11},{12,14},{13,15},{16,18},{17,... | collective-permute-start | bytes 196616 | tf_op jit(solution)/shard_map/ppermute | solution.py:22
  101.9 1.3 collective-permute-start.2
  103.3 0.5 collective-permute-done.1
  103.8 4.3 %collective-permute-done.2 = bf16[4,1,16,512]{3,2,1,0:T(8,128)(2,1)S(1)} collective-permute-done((bf16[4,1,16,512]{3,2,1,0:T(8,128)(2,1)S(1)}, bf16[4,1,16,512]{3,2,1,0:T(8,128)(2,1)S(1)}, u32[]{:S(2)}, u32[]{:S(2)}) %collective-permute-start.2) | collective-permute-done | bytes 65568 | tf_op jit(solution)/shard_map/ppermute | solution.py:23
  108.2 1.3 collective-permute-start.3
  109.5 1.3 collective-permute-start.4
  110.9 1.8 collective-permute-done.4
  112.7 0.5 pad_maximum_fusion
  113.4 0.2 pad_maximum_fusion.5
  113.7 0.2 slice.442
  113.9 0.2 broadcast_select_fusion
  114.1 0.5 pad_maximum_fusion.6
  114.6 0.6 pad_maximum_fusion.4
  115.6 1.0 copy-done.2
  116.7 0.5 copy-done
  117.3 3.9 %fusion.47 = (bf16[9,512,256]{2,1,0:T(8,128)(2,1)S(1)}, bf16[9,512,256]{2,1,0:T(8,128)(2,1)S(1)}, bf16[9,512,256]{2,1,0:T(8,128)(2,1)S(1)}) fusion(bf16[27,512,256]{2,1,0:T(8,128)(2,1)} %all-gather.3.cloned.1.call-done), kind=kLoop, calls=%fused_computation.223 | loop fusion | bytes 14155776 | tf_op jit(solution)/shard_map/slice | solution.py:52
  121.2 0.6 fusion.50
  121.9 0.9 copy-done.1
  122.7 0.6 convolution_add_fusion.4
  123.4 0.8 copy-done.3
  124.2 0.6 fusion.49
  124.9 0.1 reduce_sum.72
  125.1 40.4 %psum.30 = f32[32]{0:T(128)S(1)} all-reduce(f32[32]{0:T(128)S(1)} %reduce_sum.72), channel_id=1, replica_groups=mesh['tm'=8,'row'=2,'col'=2] {'tm','row','col'}, use_global_device_ids=true, to_apply=%region_8.9 | all-reduce | flops 32 | bytes 256 | tf_op jit(solution)/shard_map/psum | solution.py:33
  165.8 40.0 %psum.31 = f32[32]{0:T(128)S(1)} all-reduce(f32[32]{0:T(128)S(1)} %reduce_sum.75), channel_id=1, replica_groups=mesh['tm'=8,'row'=2,'col'=2] {'tm','row','col'}, use_global_device_ids=true, to_apply=%region_11.12 | all-reduce | flops 32 | bytes 256 | tf_op jit(solution)/shard_map/psum | solution.py:35
  206.1 4.2 %collective-permute-start.5 = (bf16[2,6,16,256]{3,2,1,0:T(8,128)(2,1)S(1)}, bf16[2,6,16,256]{3,2,1,0:T(8,128)(2,1)S(1)}, u32[]{:S(2)}, u32[]{:S(2)}) collective-permute-start(bf16[2,6,16,256]{3,2,1,0:T(8,128)(2,1)S(1)} %multiply_convert_fusion.1), channel_id=1, source_target_pairs={{0,4},{4,8},{8,12},{12,16},{16,20},{20,24},{24,28},{1,5},{5,9},{9,... | collective-permute-start | bytes 294920 | tf_op jit(solution)/shard_map/ppermute | solution.py:12
  210.3 5.8 %all_gather.9 = bf16[1,512,256]{2,1,0:T(8,128)(2,1)S(1)} all-gather(bf16[1,128,256]{2,1,0:T(8,128)(2,1)S(1)} %copy-done.5), channel_id=1, replica_groups=mesh['tm'=8,'row'=2,'col'=2] {'row','col'}, dimensions={1}, use_global_device_ids=true | all-gather | bytes 327680 | tf_op jit(solution)/shard_map/all_gather | solution.py:109
  216.2 3.4 %collective-permute-start.6 = (bf16[4,1,16,256]{3,2,1,0:T(8,128)(2,1)S(1)}, bf16[4,1,16,256]{3,2,1,0:T(8,128)(2,1)S(1)}, u32[]{:S(2)}, u32[]{:S(2)}) collective-permute-start(bf16[4,1,16,256]{3,2,1,0:T(8,128)(2,1)S(1)} %get-tuple-element.75), channel_id=1, source_target_pairs={{0,2},{1,3},{4,6},{5,7},{8,10},{9,11},{12,14},{13,15},{16,18},{17,... | collective-permute-start | bytes 98312 | tf_op jit(solution)/shard_map/ppermute | solution.py:22
  219.6 1.3 collective-permute-start.7
  220.9 2.2 fusion.48
  223.2 2.3 collective-permute-done.7
  225.5 1.3 collective-permute-start.8
  226.8 1.5 collective-permute-start.9
  228.3 1.6 collective-permute-done.9
  229.9 0.2 pad_maximum_fusion.2
  230.6 0.2 pad_maximum_fusion.15
  230.9 0.3 pad_maximum_fusion.13
  231.7 0.4 fusion.51
  232.1 0.4 convolution_add_fusion.2
  232.5 0.4 convolution_add_fusion.1
  232.9 0.3 copy-done.11
  233.2 0.9 fusion.2
  (125 shorter events, 3.5 us)
Async XLA Ops:
  6.5 0.9 copy-start.4
  6.5 84.6 %copy-start.10 = (f32[512]{0:T(512)S(1)}, f32[512]{0:T(512)}, u32[]{:S(2)}) copy-start(f32[512]{0:T(512)} %param.11) | copy-start | bytes 6148
  6.5 84.6 %copy-start.9 = (f32[512]{0:T(512)S(1)}, f32[512]{0:T(512)}, u32[]{:S(2)}) copy-start(f32[512]{0:T(512)} %param.12) | copy-start | bytes 6148
  6.5 110.8 %all-gather.3.cloned.1.call-start = ((), (), s32[]{:S(2)}) async-start(), calls=%async_computation | async-start | bytes 8847360 | tf_op jit(solution)/shard_map/all_gather | solution.py:105
  7.3 213.7 %all-gather.5.cloned.1.call-start = ((), (), s32[]{:S(2)}) async-start(), calls=%async_computation.1 | async-start | bytes 4423680 | tf_op jit(solution)/shard_map/all_gather | solution.py:120
  91.3 7.4 %collective-permute-start = (bf16[2,6,16,512]{3,2,1,0:T(8,128)(2,1)S(1)}, bf16[2,6,16,512]{3,2,1,0:T(8,128)(2,1)S(1)}, u32[]{:S(2)}, u32[]{:S(2)}) collective-permute-start(bf16[2,6,16,512]{3,2,1,0:T(8,128)(2,1)S(1)} %fusion.13), channel_id=1, source_target_pairs={{0,4},{4,8},{8,12},{12,16},{16,20},{20,24},{24,28},{1,5},{5,9},{9,... | collective-permute-start | bytes 589832 | tf_op jit(solution)/shard_map/ppermute | solution.py:12
  98.7 5.1 %collective-permute-start.1 = (bf16[4,1,16,512]{3,2,1,0:T(8,128)(2,1)S(1)}, bf16[4,1,16,512]{3,2,1,0:T(8,128)(2,1)S(1)}, u32[]{:S(2)}, u32[]{:S(2)}) collective-permute-start(bf16[4,1,16,512]{3,2,1,0:T(8,128)(2,1)S(1)} %get-tuple-element.44), channel_id=1, source_target_pairs={{0,2},{1,3},{4,6},{5,7},{8,10},{9,11},{12,14},{13,15},{16,18},{17,... | collective-permute-start | bytes 196616 | tf_op jit(solution)/shard_map/ppermute | solution.py:22
  101.9 6.2 %collective-permute-start.2 = (bf16[4,1,16,512]{3,2,1,0:T(8,128)(2,1)S(1)}, bf16[4,1,16,512]{3,2,1,0:T(8,128)(2,1)S(1)}, u32[]{:S(2)}, u32[]{:S(2)}) collective-permute-start(bf16[4,1,16,512]{3,2,1,0:T(8,128)(2,1)S(1)} %get-tuple-element.45), channel_id=1, source_target_pairs={{2,0},{3,1},{6,4},{7,5},{10,8},{11,9},{14,12},{15,13},{18,16},{19,... | collective-permute-start | bytes 196616 | tf_op jit(solution)/shard_map/ppermute | solution.py:23
  108.2 2.6 %collective-permute-start.3 = (bf16[4,8,1,512]{3,2,1,0:T(2,128)(2,1)S(1)}, bf16[4,8,1,512]{3,2,1,0:T(2,128)(2,1)S(1)}, u32[]{:S(2)}, u32[]{:S(2)}) collective-permute-start(bf16[4,8,1,512]{3,2,1,0:T(2,128)(2,1)S(1)} %get-tuple-element.40), channel_id=1, source_target_pairs={{0,1},{2,3},{4,5},{6,7},{8,9},{10,11},{12,13},{14,15},{16,17},{18,... | collective-permute-start | bytes 98312 | tf_op jit(solution)/shard_map/ppermute | solution.py:22
  109.5 3.1 %collective-permute-start.4 = (bf16[4,8,1,512]{3,2,1,0:T(2,128)(2,1)S(1)}, bf16[4,8,1,512]{3,2,1,0:T(2,128)(2,1)S(1)}, u32[]{:S(2)}, u32[]{:S(2)}) collective-permute-start(bf16[4,8,1,512]{3,2,1,0:T(2,128)(2,1)S(1)} %get-tuple-element.41), channel_id=1, source_target_pairs={{1,0},{3,2},{5,4},{7,6},{9,8},{11,10},{13,12},{15,14},{17,16},{19,... | collective-permute-start | bytes 98312 | tf_op jit(solution)/shard_map/ppermute | solution.py:23
  115.4 1.2 copy-start.2
  115.6 1.7 copy-start
  121.2 1.5 copy-start.1
  122.7 1.5 copy-start.3
  122.7 1.5 copy-start.6
  124.2 81.8 %copy-start.7 = (f32[256]{0:T(256)S(1)}, f32[256]{0:T(256)}, u32[]{:S(2)}) copy-start(f32[256]{0:T(256)} %param.17) | copy-start | bytes 3076
  124.2 81.8 %copy-start.8 = (f32[256]{0:T(256)S(1)}, f32[256]{0:T(256)}, u32[]{:S(2)}) copy-start(f32[256]{0:T(256)} %param.16) | copy-start | bytes 3076
  124.2 86.1 %copy-start.5 = (bf16[1,128,256]{2,1,0:T(8,128)(2,1)S(1)}, bf16[1,128,256]{2,1,0:T(8,128)(2,1)}, u32[]{:S(2)}) copy-start(bf16[1,128,256]{2,1,0:T(8,128)(2,1)} %param.15) | copy-start | bytes 196612
  206.1 10.0 %collective-permute-start.5 = (bf16[2,6,16,256]{3,2,1,0:T(8,128)(2,1)S(1)}, bf16[2,6,16,256]{3,2,1,0:T(8,128)(2,1)S(1)}, u32[]{:S(2)}, u32[]{:S(2)}) collective-permute-start(bf16[2,6,16,256]{3,2,1,0:T(8,128)(2,1)S(1)} %multiply_convert_fusion.1), channel_id=1, source_target_pairs={{0,4},{4,8},{8,12},{12,16},{16,20},{20,24},{24,28},{1,5},{5,9},{9,... | collective-permute-start | bytes 294920 | tf_op jit(solution)/shard_map/ppermute | solution.py:12
  216.2 7.0 %collective-permute-start.6 = (bf16[4,1,16,256]{3,2,1,0:T(8,128)(2,1)S(1)}, bf16[4,1,16,256]{3,2,1,0:T(8,128)(2,1)S(1)}, u32[]{:S(2)}, u32[]{:S(2)}) collective-permute-start(bf16[4,1,16,256]{3,2,1,0:T(8,128)(2,1)S(1)} %get-tuple-element.75), channel_id=1, source_target_pairs={{0,2},{1,3},{4,6},{5,7},{8,10},{9,11},{12,14},{13,15},{16,18},{17,... | collective-permute-start | bytes 98312 | tf_op jit(solution)/shard_map/ppermute | solution.py:22
  219.6 5.8 %collective-permute-start.7 = (bf16[4,1,16,256]{3,2,1,0:T(8,128)(2,1)S(1)}, bf16[4,1,16,256]{3,2,1,0:T(8,128)(2,1)S(1)}, u32[]{:S(2)}, u32[]{:S(2)}) collective-permute-start(bf16[4,1,16,256]{3,2,1,0:T(8,128)(2,1)S(1)} %get-tuple-element.76), channel_id=1, source_target_pairs={{2,0},{3,1},{6,4},{7,5},{10,8},{11,9},{14,12},{15,13},{18,16},{19,... | collective-permute-start | bytes 98312 | tf_op jit(solution)/shard_map/ppermute | solution.py:23
  225.5 2.8 %collective-permute-start.8 = (bf16[4,8,1,256]{3,2,1,0:T(2,128)(2,1)S(1)}, bf16[4,8,1,256]{3,2,1,0:T(2,128)(2,1)S(1)}, u32[]{:S(2)}, u32[]{:S(2)}) collective-permute-start(bf16[4,8,1,256]{3,2,1,0:T(2,128)(2,1)S(1)} %get-tuple-element.73), channel_id=1, source_target_pairs={{0,1},{2,3},{4,5},{6,7},{8,9},{10,11},{12,13},{14,15},{16,17},{18,... | collective-permute-start | bytes 49160 | tf_op jit(solution)/shard_map/ppermute | solution.py:22
  226.8 3.1 %collective-permute-start.9 = (bf16[4,8,1,256]{3,2,1,0:T(2,128)(2,1)S(1)}, bf16[4,8,1,256]{3,2,1,0:T(2,128)(2,1)S(1)}, u32[]{:S(2)}, u32[]{:S(2)}) collective-permute-start(bf16[4,8,1,256]{3,2,1,0:T(2,128)(2,1)S(1)} %get-tuple-element.74), channel_id=1, source_target_pairs={{1,0},{3,2},{5,4},{7,6},{9,8},{11,10},{13,12},{15,14},{17,16},{19,... | collective-permute-start | bytes 49160 | tf_op jit(solution)/shard_map/ppermute | solution.py:23
  232.5 0.7 copy-start.11
Sparse Core Ops, SparseCore 0:
  8.9 54.9 all-gather.2
  103.4 33.4 all-gather.4
where the time goes:
time: 242 us; the launch traced here: 241 us
  blocking collectives  169 us (70%)
  starting transfers between devices  23 us (10%)
  waiting for transfers between devices  14.5 us (6%)
  between operations  14.3 us (6%)
  local copies, waits for them, and re-layouts  11.7 us (5%)
  other arithmetic  4.53 us (2%)
  matrix products  3.96 us (2%)
    psum x2, blocking collectives, group_silu(): mean = lax.psum(jnp.sum(grouped, axis=(0, 2)), ('tm', 'row', 'col')) / count  82.7 us
    psum x2, blocking collectives, group_silu(): lax.psum(jnp.sum(centred * centred, axis=(0, 2)), ('tm', 'row', 'col'))  80.4 us
    ppermute x4, waiting for transfers between devices, with_halo(): after = lax.ppermute(leading, axis, down)  9.93 us
    ppermute x4, starting transfers between devices, with_halo(): before = lax.ppermute(last, axis, up)  9.24 us
    ppermute x2, starting transfers between devices, passed_along(): return lax.ppermute(block, axis, route)  8.38 us
    slice x2, local copies, waits for them, and re-layouts, conv_taps(): flat_weight = weight[9 * dt:9 * dt + 9].reshape(9 * chans, weight.shape[2])  6.09 us
    all_gather x1, blocking collectives, per_device(): lax.all_gather(skip_weight, ('row', 'col'), axis=1, tiled=True)[0]  5.82 us
    ppermute x4, starting transfers between devices, with_halo(): after = lax.ppermute(leading, axis, down)  5.35 us
  transfers between devices with their start and end apart: 12, of which 6 were waited for; matrix products, arithmetic and copies ran while one was open for 5% of the time, Pallas kernels for 0%

commit v1 on v0

--- a/solution.py
+++ b/solution.py
@@ -1,6 +1,10 @@
+import functools
+
 import jax
 import jax.numpy as jnp
 from jax import lax
+from jax.experimental import pallas as pl
+from jax.experimental.pallas import tpu as pltpu
 from jax.sharding import PartitionSpec as P
 
 GROUPS = 32
@@ -76,7 +80,7 @@
     return jnp.concatenate([left, padded[:, :, 1:-1], right], axis=2)
 
 
-def per_device(
+def per_device_gathered(
     features,
     gn1_gain,
     gn1_bias,
@@ -123,6 +127,431 @@
     return block_out.reshape(frames, rows, cols, chans_out)
 
 
+MESH = pl.DeviceIdType.MESH
+LANES = 128
+
+
+def lane_of(shape):
+    return lax.broadcasted_iota(jnp.int32, shape, len(shape) - 1)
+
+
+def silu(a):
+    half = 0.5 * a
+    return half + half * jnp.tanh(half)
+
+
+def lane_stats(x):
+    mean = jnp.sum(x, axis=0, keepdims=True) * (1.0 / x.shape[0])
+    spread = jnp.sum((x - mean) ** 2, axis=0, keepdims=True)
+    row = lax.broadcasted_iota(jnp.int32, (8, LANES), 0)
+    return jnp.where(row == 0, mean, jnp.where(row == 1, spread, 0.0))
+
+
+def group_stats(stats, same, lanes, count):
+    devices = stats.shape[0]
+    means, spreads = stats[:, 0:1, :], stats[:, 1:2, :]
+    mean = jnp.sum(means, axis=0) * (1.0 / devices)
+    spread = jnp.sum(spreads, axis=0) + count * jnp.sum((means - mean[None]) ** 2, axis=0)
+    mean = jnp.broadcast_to(mean, (8, LANES))
+    group_mean = (
+        jnp.dot(mean, same, precision=lax.Precision.HIGHEST, preferred_element_type=jnp.float32)
+        * (1.0 / lanes)
+    )
+    spread = spread + (count * devices) * (mean - group_mean) ** 2
+    total = jnp.dot(
+        spread, same, precision=lax.Precision.HIGHEST, preferred_element_type=jnp.float32
+    )
+    inv = lax.rsqrt(total * (1.0 / (count * devices * lanes)) + 1e-6)
+    return group_mean[0:1], inv[0:1]
+
+
+def side_shifts(h, cols):
+    col = lax.broadcasted_iota(jnp.int32, h.shape, 0) & (cols - 1)
+    length = h.shape[0]
+    left = jnp.where(col == 0, h, pltpu.roll(h, 1, 0))
+    right = jnp.where(col == cols - 1, h, pltpu.roll(h, length - 1, 0))
+    return left, right
+
+
+def block_kernel(
+    sizes,
+    feat, gain1, shift1, w1, bias1, wskip, gain2, shift2, w2, bias2,
+    out,
+    xall, w1v, wsv, wa, wb, xp1, xp2, part1, send1, recv1, stat1, stat2,
+    midbf, prevbf, scut, part2, send2, recv2,
+    w_sem, own_sem, fs_sem, fr_sem, fps_sem, fpr_sem,
+    s1s_sem, s1r_sem, s2s_sem, s2r_sem, r1s_sem, r1r_sem, r2s_sem, r2r_sem,
+    ps_sem, pr_sem,
+):
+    slabs, nrow, ncol, rows, cols, per1, per2 = sizes
+    n = nrow * ncol
+    height, width = nrow * rows, ncol * cols
+    area = height * width
+    t = lax.axis_index("tm")
+    r = lax.axis_index("row")
+    c = lax.axis_index("col")
+    me = r * ncol + c
+
+    def place(i):
+        return lax.div(i, ncol), lax.rem(i, ncol)
+
+    def ident(ti, i):
+        ri, ci = place(i)
+        return {"tm": ti, "row": ri, "col": ci}
+
+    def member(delta):
+        return lax.rem(me + delta, n)
+
+    def slab(delta):
+        return lax.rem(t + delta, slabs)
+
+    loads = [
+        pltpu.make_async_copy(w1, w1v, w_sem.at[0]),
+        pltpu.make_async_copy(wskip, wsv, w_sem.at[1]),
+    ]
+    for dt in range(3):
+        lo = dt * per2
+        loads.append(
+            pltpu.make_async_copy(w2.at[dt], wa.at[:, lo : lo + per2, :], w_sem.at[2 + dt])
+        )
+        loads.append(
+            pltpu.make_async_copy(
+                w2.at[dt], wb.at[:, lo + per2 : lo + 2 * per2, :], w_sem.at[5 + dt]
+            )
+        )
+
+    def window(frame0, i):
+        ri, ci = place(i)
+        top = ri * rows
+        left = pl.multiple_of(ci * cols, cols)
+        return xall.at[frame0 : frame0 + 2, pl.ds(top, rows), pl.ds(left, cols), :]
+
+    def chunk(i):
+        return feat.at[:, :, :, pl.ds(pl.multiple_of(i * LANES, LANES), LANES)]
+
+    own = pltpu.make_async_copy(chunk(me), window(2, me), own_sem)
+    own.start()
+
+    barrier = pltpu.get_barrier_semaphore()
+    for delta in range(1, n):
+        pl.semaphore_signal(barrier, inc=1, device_id=ident(t, member(delta)), device_id_type=MESH)
+    for delta in range(1, slabs):
+        pl.semaphore_signal(barrier, inc=1, device_id=ident(slab(delta), me), device_id_type=MESH)
+
+    @pl.when(t > 0)
+    def _():
+        for delta in range(1, n):
+            pl.semaphore_signal(
+                barrier, inc=1, device_id=ident(t - 1, member(delta)), device_id_type=MESH
+            )
+
+    pl.semaphore_wait(barrier, jnp.where(t < slabs - 1, 2 * (n - 1), n - 1) + slabs - 1)
+
+    def feat_copy(source, target):
+        return pltpu.make_async_remote_copy(
+            src_ref=chunk(target), dst_ref=window(2, source),
+            send_sem=fs_sem.at[target], recv_sem=fr_sem.at[source],
+            device_id=ident(t, target), device_id_type=MESH,
+        )
+
+    def feat_next(source, target, to):
+        return pltpu.make_async_remote_copy(
+            src_ref=chunk(target), dst_ref=window(0, source),
+            send_sem=fps_sem.at[target], recv_sem=fpr_sem.at[source],
+            device_id=ident(to, target), device_id_type=MESH,
+        )
+
+    for delta in range(1, n):
+        feat_copy(me, member(delta)).start()
+
+    @pl.when(t < slabs - 1)
+    def _():
+        for delta in range(n):
+            feat_next(me, member(delta), t + 1).start()
+
+    for load in loads:
+        load.start()
+    wa[:, 3 * per2 :, :] = jnp.zeros((9, 4 * per2 - 3 * per2, wa.shape[2]), wa.dtype)
+    wb[:, :per2, :] = jnp.zeros((9, per2, wb.shape[2]), wb.dtype)
+
+    lane = lane_of((8, LANES))
+    lane_in = lax.broadcasted_iota(jnp.int32, (LANES, LANES), 0)
+    lane_to = lane_of((LANES, LANES))
+    size1 = per1 // (GROUPS // n)
+    size2 = per2 // (GROUPS // n)
+    same1 = (lane_in // size1 == lane_to // size1).astype(jnp.float32)
+    same2 = ((lane_in % per2) // size2 == (lane_to % per2) // size2).astype(jnp.float32)
+
+    def own_full(ref):
+        result = ref[0:1, 0:LANES]
+        for d in range(1, n):
+            result = jnp.where(me == d, ref[0:1, d * LANES : (d + 1) * LANES], result)
+        return result
+
+    def own_twice(ref):
+        result = jnp.zeros((8, LANES), jnp.float32)
+        for d in range(n):
+            k = d // 2 * LANES
+            seg = jnp.broadcast_to(ref[0:1, k : k + LANES], (8, LANES))
+            turned = pltpu.roll(seg, per2, 1)
+            twice = jnp.where((lane < per2) == (d % 2 == 0), seg, turned)
+            result = jnp.where(me == d, twice, result)
+        return result[0:1]
+
+    g1, b1 = own_full(gain1), own_full(shift1)
+    g2, b2, c1 = own_twice(gain2), own_twice(shift2), own_twice(bias1)
+
+    def stat_copy(buf, source, target, ssem, rsem):
+        return pltpu.make_async_remote_copy(
+            src_ref=buf.at[source], dst_ref=buf.at[source],
+            send_sem=ssem.at[target], recv_sem=rsem.at[source],
+            device_id=ident(target, me), device_id_type=MESH,
+        )
+
+    own.wait()
+    for delta in range(1, n):
+        feat_copy(member(delta), me).wait_recv()
+    raw = xall[2:4].reshape(2 * area, LANES).astype(jnp.float32)
+    stat1[t] = lane_stats(raw)
+    for delta in range(1, slabs):
+        stat_copy(stat1, t, slab(delta), s1s_sem, s1r_sem).start()
+
+    loads[1].wait()
+    for f in range(2):
+        x = xall[2 + f].reshape(area, LANES)
+        scut[f] = jnp.dot(x, wsv[...], preferred_element_type=jnp.float32)
+
+    @pl.when(t > 0)
+    def _():
+        for delta in range(n):
+            feat_next(member(delta), me, t).wait_recv()
+
+    @pl.when(t == 0)
+    def _():
+        xall[0] = xall[2]
+        xall[1] = xall[2]
+
+    for delta in range(1, slabs):
+        stat_copy(stat1, slab(delta), t, s1s_sem, s1r_sem).wait_recv()
+    mean, inv = group_stats(stat1[...], same1, size1, float(2 * area))
+    scale = inv * g1
+    for f in range(4):
+        x = xall[f].reshape(area, LANES).astype(jnp.float32)
+        h = silu((x - mean) * scale + b1)
+        left, right = side_shifts(h, width)
+        for dx, part in enumerate((left, h, right)):
+            part = part.astype(jnp.bfloat16).reshape(height, width, LANES)
+            lanes = slice(dx * LANES, (dx + 1) * LANES)
+            xp1[f, 1 : height + 1, :, lanes] = part
+            xp1[f, 0, :, lanes] = part[0]
+            xp1[f, height + 1, :, lanes] = part[height - 1]
+
+    loads[0].wait()
+    depth = 9 * LANES
+    firsts = []
+    for f in range(2):
+        total = None
+        for dt in range(3):
+            lhs = jnp.concatenate(
+                [xp1[f + dt, dy : dy + height].reshape(area, 3 * LANES) for dy in range(3)], axis=1
+            )
+            term = jnp.dot(
+                lhs, w1v[dt * depth : (dt + 1) * depth, :], preferred_element_type=jnp.float32
+            )
+            total = term if total is None else total + term
+        firsts.append(total)
+    wide = lane_of((area, LANES))
+    for d in range(n):
+        k = d // 2 * LANES
+        one, two = firsts[0][:, k : k + LANES], firsts[1][:, k : k + LANES]
+        if d % 2 == 0:
+            packed = jnp.where(wide < per2, one, pltpu.roll(two, per2, 1))
+        else:
+            packed = jnp.where(wide < per2, pltpu.roll(one, per2, 1), two)
+        part1[d] = packed
+        send1[d] = packed.astype(jnp.bfloat16)
+
+    def sum_copy(src, dst, source, target, ssem, rsem):
+        return pltpu.make_async_remote_copy(
+            src_ref=src.at[target], dst_ref=dst.at[source],
+            send_sem=ssem.at[target], recv_sem=rsem.at[source],
+            device_id=ident(t, target), device_id_type=MESH,
+        )
+
+    for delta in range(1, n):
+        sum_copy(send1, recv1, me, member(delta), r1s_sem, r1r_sem).start()
+    middle = part1[me] + c1
+    for delta in range(1, n):
+        source = member(delta)
+        sum_copy(send1, recv1, source, me, r1s_sem, r1r_sem).wait_recv()
+        middle = middle + recv1[source].astype(jnp.float32)
+
+    midbf[...] = middle.astype(jnp.bfloat16)
+
+    def mid_copy(to):
+        return pltpu.make_async_remote_copy(
+            src_ref=midbf, dst_ref=prevbf, send_sem=ps_sem, recv_sem=pr_sem,
+            device_id=ident(to, me), device_id_type=MESH,
+        )
+
+    stat2[t] = lane_stats(middle)
+    for delta in range(1, slabs):
+        stat_copy(stat2, t, slab(delta), s2s_sem, s2r_sem).start()
+
+    @pl.when(t < slabs - 1)
+    def _():
+        mid_copy(t + 1).start()
+
+    part1[0] = middle
+
+    @pl.when(t > 0)
+    def _():
+        mid_copy(t).wait_recv()
+        part1[1] = prevbf[...].astype(jnp.float32)
+
+    @pl.when(t == 0)
+    def _():
+        part1[1] = jnp.where(wide < per2, middle, pltpu.roll(middle, per2, 1))
+
+    for delta in range(1, slabs):
+        stat_copy(stat2, slab(delta), t, s2s_sem, s2r_sem).wait_recv()
+    mean, inv = group_stats(stat2[...], same2, 2 * size2, float(area))
+    scale = inv * g2
+    for i in range(2):
+        h = silu((part1[1 - i] - mean) * scale + b2)
+        left, right = side_shifts(h, width)
+        for dx, part in enumerate((left, h, right)):
+            part = part.astype(jnp.bfloat16).reshape(height, width, LANES)
+            lanes = slice((2 * dx + i) * LANES, (2 * dx + i + 1) * LANES)
+            xp2[1 : height + 1, :, lanes] = part
+            xp2[0, :, lanes] = part[0]
+            xp2[height + 1, :, lanes] = part[height - 1]
+
+    for load in loads[2:]:
+        load.wait()
+    for f, weight in enumerate((wa, wb)):
+        total = scut[f]
+        for dy in range(3):
+            lhs = xp2[dy : dy + height].reshape(area, 6 * LANES)
+            rhs = weight[3 * dy : 3 * dy + 3].reshape(6 * LANES, weight.shape[2])
+            total = total + jnp.dot(lhs, rhs, preferred_element_type=jnp.float32)
+        total = total.reshape(height, width, weight.shape[2])
+        for d in range(n):
+            ri, ci = d // ncol, d % ncol
+            piece = total[ri * rows : (ri + 1) * rows, ci * cols : (ci + 1) * cols]
+            part2[d, f] = piece
+            send2[d, f] = piece.astype(jnp.bfloat16)
+
+    for delta in range(1, n):
+        sum_copy(send2, recv2, me, member(delta), r2s_sem, r2r_sem).start()
+    result = part2[me] + bias2[...].reshape(1, 1, 1, -1)
+    for delta in range(1, n):
+        source = member(delta)
+        sum_copy(send2, recv2, source, me, r2s_sem, r2r_sem).wait_recv()
+        result = result + recv2[source].astype(jnp.float32)
+    out[...] = result.astype(out.dtype)
+
+    for delta in range(1, n):
+        target = member(delta)
+        feat_copy(me, target).wait_send()
+        sum_copy(send1, recv1, me, target, r1s_sem, r1r_sem).wait_send()
+        sum_copy(send2, recv2, me, target, r2s_sem, r2r_sem).wait_send()
+    for delta in range(1, slabs):
+        stat_copy(stat1, t, slab(delta), s1s_sem, s1r_sem).wait_send()
+        stat_copy(stat2, t, slab(delta), s2s_sem, s2r_sem).wait_send()
+
+    @pl.when(t < slabs - 1)
+    def _():
+        for delta in range(n):
+            feat_next(me, member(delta), t + 1).wait_send()
+        mid_copy(t + 1).wait_send()
+
+
+def per_device(
+    features,
+    gn1_gain,
+    gn1_bias,
+    conv1_weight,
+    conv1_bias,
+    skip_weight,
+    gn2_gain,
+    gn2_bias,
+    conv2_weight,
+    conv2_bias,
+):
+    frames, rows, cols, chans_in = features.shape
+    per1, per2 = conv1_weight.shape[1], conv2_weight.shape[1]
+    chans_out = conv1_weight.shape[2]
+    slabs, nrow, ncol = (lax.axis_size(a) for a in ("tm", "row", "col"))
+    n = nrow * ncol
+    height, width = nrow * rows, ncol * cols
+    area = height * width
+    fits = frames == 2 and per1 == LANES and 2 * per2 == LANES and cols % 16 == 0
+    fits = fits and width & (width - 1) == 0 and GROUPS % n == 0
+    if not fits:
+        return per_device_gathered(
+            features, gn1_gain, gn1_bias, conv1_weight, conv1_bias, skip_weight,
+            gn2_gain, gn2_bias, conv2_weight, conv2_bias,
+        )
+    bf16, f32 = jnp.bfloat16, jnp.float32
+    vmem, dma = pltpu.VMEM, pltpu.SemaphoreType.DMA
+    scratch = [
+        vmem((4, height, width, LANES), bf16),
+        vmem((27 * per1, chans_out), bf16),
+        vmem((per1, chans_out), bf16),
+        vmem((9, 4 * per2, chans_out), bf16),
+        vmem((9, 4 * per2, chans_out), bf16),
+        vmem((4, height + 2, width, 3 * LANES), bf16),
+        vmem((height + 2, width, 6 * LANES), bf16),
+        vmem((n, area, LANES), f32),
+        vmem((n, area, LANES), bf16),
+        vmem((n, area, LANES), bf16),
+        vmem((slabs, 8, LANES), f32),
+        vmem((slabs, 8, LANES), f32),
+        vmem((area, LANES), bf16),
+        vmem((area, LANES), bf16),
+        vmem((2, area, chans_out), f32),
+        vmem((n, 2, rows, cols, chans_out), f32),
+        vmem((n, 2, rows, cols, chans_out), bf16),
+        vmem((n, 2, rows, cols, chans_out), bf16),
+        dma((8,)), dma, dma((n,)), dma((n,)), dma((n,)), dma((n,)),
+        dma((slabs,)), dma((slabs,)), dma((slabs,)), dma((slabs,)),
+        dma((n,)), dma((n,)), dma((n,)), dma((n,)),
+        dma, dma,
+    ]
+    anywhere = pl.BlockSpec(memory_space=pl.ANY)
+    inside = pl.BlockSpec(memory_space=pltpu.VMEM)
+    sizes = (slabs, nrow, ncol, rows, cols, per1, per2)
+    flops = 2 * 2 * area * chans_out * (28 * per1 + 27 * per2)
+    return pl.pallas_call(
+        functools.partial(block_kernel, sizes),
+        out_shape=jax.ShapeDtypeStruct((frames, rows, cols, chans_out), bf16),
+        in_specs=[
+            anywhere, inside, inside, anywhere, inside, anywhere, inside, inside, anywhere, inside,
+        ],
+        out_specs=inside,
+        scratch_shapes=scratch,
+        compiler_params=pltpu.CompilerParams(
+            collective_id=0, has_side_effects=True, vmem_limit_bytes=48 * 1024 * 1024
+        ),
+        cost_estimate=pl.CostEstimate(
+            flops=flops, bytes_accessed=4 * 1024 * 1024, transcendentals=6 * area * LANES
+        ),
+        name="residual_block",
+    )(
+        features,
+        gn1_gain.reshape(1, -1),
+        gn1_bias.reshape(1, -1),
+        conv1_weight.reshape(27 * per1, chans_out),
+        conv1_bias.reshape(1, -1),
+        skip_weight.reshape(per1, chans_out),
+        gn2_gain.reshape(1, -1),
+        gn2_bias.reshape(1, -1),
+        conv2_weight.reshape(3, 9, per2, chans_out),
+        conv2_bias.reshape(1, -1),
+    )
+
+
 def solution(mesh):
     in_specs = (
         P("tm", "row", "col", None),

time: 242 us -> 43.7 us (0.18)
  the two profiles are of different devices: /device:TPU:0 before, /device:TPU:1 now
where the time goes in v1:
time: 43.7 us; the launch traced here: 43.4 us
  Pallas kernels  34.2 us (78%)
  local copies, waits for them, and re-layouts  9.13 us (21%)
    pallas_call x1, Pallas kernels, per_device(): pl.pallas_call(functools.partial(block_kernel, sizes), out_shape=jax.Shap...  34.2 us
    unnamed x21, local copies, waits for them, and re-layouts  9.13 us

profile of v1, /device:TPU:1, one launch (start us, length us, event | category | flops | bytes accessed | tf_op | source)
XLA Modules:
  0.0 43.4 jit_solution(18404128911711861290)
XLA Ops:
  0.0 0.0 copy-start
  0.0 1.5 %copy-done = bf16[27,128,256]{2,1,0:T(8,128)(2,1)S(1)} copy-done((bf16[27,128,256]{2,1,0:T(8,128)(2,1)S(1)}, bf16[27,128,256]{2,1,0:T(8,128)(2,1)}, u32[]{:S(2)}) %copy-start) | copy-done | bytes 1769496
  1.5 0.0 copy-start.1
  1.5 1.2 %copy-done.1 = bf16[27,64,256]{2,1,0:T(8,128)(2,1)S(1)} copy-done((bf16[27,64,256]{2,1,0:T(8,128)(2,1)S(1)}, bf16[27,64,256]{2,1,0:T(8,128)(2,1)}, u32[]{:S(2)}) %copy-start.1) | copy-done | bytes 884760
  2.6 0.0 copy-start.2
  2.6 0.9 %copy-done.2 = bf16[2,6,16,512]{3,2,1,0:T(8,128)(2,1)S(1)} copy-done((bf16[2,6,16,512]{3,2,1,0:T(8,128)(2,1)S(1)}, bf16[2,6,16,512]{3,2,1,0:T(8,128)(2,1)}, u32[]{:S(2)}) %copy-start.2) | copy-done | bytes 196632
  3.6 0.0 copy-start.3
  3.6 0.8 %copy-done.3 = bf16[1,128,256]{2,1,0:T(8,128)(2,1)S(1)} copy-done((bf16[1,128,256]{2,1,0:T(8,128)(2,1)S(1)}, bf16[1,128,256]{2,1,0:T(8,128)(2,1)}, u32[]{:S(2)}) %copy-start.3) | copy-done | bytes 65560
  4.4 0.0 copy-start.4
  4.4 0.7 %copy-done.4 = f32[512]{0:T(512)S(1)} copy-done((f32[512]{0:T(512)S(1)}, f32[512]{0:T(512)}, u32[]{:S(2)}) %copy-start.4) | copy-done | bytes 2072
  5.1 0.0 copy-start.5
  5.1 0.7 %copy-done.5 = f32[512]{0:T(512)S(1)} copy-done((f32[512]{0:T(512)S(1)}, f32[512]{0:T(512)}, u32[]{:S(2)}) %copy-start.5) | copy-done | bytes 2072
  5.8 0.0 copy-start.6
  5.8 0.7 %copy-done.6 = f32[256]{0:T(256)S(1)} copy-done((f32[256]{0:T(256)S(1)}, f32[256]{0:T(256)}, u32[]{:S(2)}) %copy-start.6) | copy-done | bytes 1048
  6.5 0.0 copy-start.7
  6.5 0.7 %copy-done.7 = f32[256]{0:T(256)S(1)} copy-done((f32[256]{0:T(256)S(1)}, f32[256]{0:T(256)}, u32[]{:S(2)}) %copy-start.7) | copy-done | bytes 1048
  7.1 0.0 copy-start.8
  7.1 0.7 %copy-done.8 = f32[256]{0:T(256)S(1)} copy-done((f32[256]{0:T(256)S(1)}, f32[256]{0:T(256)}, u32[]{:S(2)}) %copy-start.8) | copy-done | bytes 1048
  7.8 0.0 copy-start.9
  7.8 0.7 %copy-done.9 = f32[256]{0:T(256)S(1)} copy-done((f32[256]{0:T(256)S(1)}, f32[256]{0:T(256)}, u32[]{:S(2)}) %copy-start.9) | copy-done | bytes 1048
  8.5 34.2 %residual_block.1 = bf16[2,6,16,256]{3,2,1,0:T(8,128)(2,1)S(1)} custom-call(bf16[2,6,16,512]{3,2,1,0:T(8,128)(2,1)S(1)} %copy-done.2, f32[1,512]{1,0:T(1,128)S(1)} %bitcast.12, f32[1,512]{1,0:T(1,128)S(1)} %bitcast.13, bf16[3456,256]{1,0:T(8,128)(2,1)S(1)} %bitcast.9, f32[1,256]{1,0:T(1,128)S(1)} %bitcast.14, bf16[128,256]{1,0:T(8,128)(2,1)S(1)} %bitcast.11, ...), custom_call_target="tpu_custom_call" | custom-call | flops 2088763392 | bytes 4194304 | tf_op jit(solution)/shard_map/residual_block/pallas_call | solution.py:526
  42.7 0.6 %copy.12 = bf16[2,6,16,256]{3,2,1,0:T(8,128)(2,1)} copy(bf16[2,6,16,256]{3,2,1,0:T(8,128)(2,1)S(1)} %residual_block.1) | data formatting | bytes 196608
Async XLA Ops:
  0.0 1.5 %copy-start = (bf16[27,128,256]{2,1,0:T(8,128)(2,1)S(1)}, bf16[27,128,256]{2,1,0:T(8,128)(2,1)}, u32[]{:S(2)}) copy-start(bf16[27,128,256]{2,1,0:T(8,128)(2,1)} %param.13) | copy-start | bytes 5308420
  1.5 1.2 %copy-start.1 = (bf16[27,64,256]{2,1,0:T(8,128)(2,1)S(1)}, bf16[27,64,256]{2,1,0:T(8,128)(2,1)}, u32[]{:S(2)}) copy-start(bf16[27,64,256]{2,1,0:T(8,128)(2,1)} %param.18) | copy-start | bytes 2654212
  2.6 0.9 %copy-start.2 = (bf16[2,6,16,512]{3,2,1,0:T(8,128)(2,1)S(1)}, bf16[2,6,16,512]{3,2,1,0:T(8,128)(2,1)}, u32[]{:S(2)}) copy-start(bf16[2,6,16,512]{3,2,1,0:T(8,128)(2,1)} %feat.1) | copy-start | bytes 589828
  3.6 0.8 %copy-start.3 = (bf16[1,128,256]{2,1,0:T(8,128)(2,1)S(1)}, bf16[1,128,256]{2,1,0:T(8,128)(2,1)}, u32[]{:S(2)}) copy-start(bf16[1,128,256]{2,1,0:T(8,128)(2,1)} %param.15) | copy-start | bytes 196612
  4.4 0.7 %copy-start.4 = (f32[512]{0:T(512)S(1)}, f32[512]{0:T(512)}, u32[]{:S(2)}) copy-start(f32[512]{0:T(512)} %param.11) | copy-start | bytes 6148
  5.1 0.7 %copy-start.5 = (f32[512]{0:T(512)S(1)}, f32[512]{0:T(512)}, u32[]{:S(2)}) copy-start(f32[512]{0:T(512)} %param.12) | copy-start | bytes 6148
  5.8 0.7 %copy-start.6 = (f32[256]{0:T(256)S(1)}, f32[256]{0:T(256)}, u32[]{:S(2)}) copy-start(f32[256]{0:T(256)} %param.14) | copy-start | bytes 3076
  6.5 0.7 %copy-start.7 = (f32[256]{0:T(256)S(1)}, f32[256]{0:T(256)}, u32[]{:S(2)}) copy-start(f32[256]{0:T(256)} %param.16) | copy-start | bytes 3076
  7.1 0.7 %copy-start.8 = (f32[256]{0:T(256)S(1)}, f32[256]{0:T(256)}, u32[]{:S(2)}) copy-start(f32[256]{0:T(256)} %param.17) | copy-start | bytes 3076
  7.8 0.7 %copy-start.9 = (f32[256]{0:T(256)S(1)}, f32[256]{0:T(256)}, u32[]{:S(2)}) copy-start(f32[256]{0:T(256)} %param.19) | copy-start | bytes 3076

commit v2 on v1

--- a/solution.py
+++ b/solution.py
@@ -175,11 +175,11 @@
 
 def block_kernel(
     sizes,
-    feat, gain1, shift1, w1, bias1, wskip, gain2, shift2, w2, bias2,
+    feat, gain1_hbm, shift1_hbm, w1, bias1_hbm, wskip, gain2_hbm, shift2_hbm, w2, bias2_hbm,
     out,
-    xall, w1v, wsv, wa, wb, xp1, xp2, part1, send1, recv1, stat1, stat2,
-    midbf, prevbf, scut, part2, send2, recv2,
-    w_sem, own_sem, fs_sem, fr_sem, fps_sem, fpr_sem,
+    gain1, shift1, bias1, gain2, shift2, bias2, xall, w1v, wsv, wa, wb, xp1, xp2, acc, part1, send1, recv1, stat1, stat2,
+    mids, midbf, prevbf, scut, part2, send2, recv2,
+    w_sem, p_sem, own_sem, fs_sem, fr_sem, fps_sem, fpr_sem,
     s1s_sem, s1r_sem, s2s_sem, s2r_sem, r1s_sem, r1r_sem, r2s_sem, r2r_sem,
     ps_sem, pr_sem,
 ):
@@ -200,7 +200,7 @@
         return {"tm": ti, "row": ri, "col": ci}
 
     def member(delta):
-        return lax.rem(me + delta, n)
+        return lax.rem(r + delta // ncol, nrow) * ncol + lax.rem(c + delta % ncol, ncol)
 
     def slab(delta):
         return lax.rem(t + delta, slabs)
@@ -220,6 +220,16 @@
             )
         )
 
+    params = [
+        pltpu.make_async_copy(source, target, p_sem.at[i])
+        for i, (source, target) in enumerate(
+            (
+                (gain1_hbm, gain1), (shift1_hbm, shift1), (bias1_hbm, bias1),
+                (gain2_hbm, gain2), (shift2_hbm, shift2), (bias2_hbm, bias2),
+            )
+        )
+    ]
+
     def window(frame0, i):
         ri, ci = place(i)
         top = ri * rows
@@ -245,6 +255,10 @@
                 barrier, inc=1, device_id=ident(t - 1, member(delta)), device_id_type=MESH
             )
 
+    for load in params + loads:
+        load.start()
+    wa[:, 3 * per2 :, :] = jnp.zeros((9, 4 * per2 - 3 * per2, wa.shape[2]), wa.dtype)
+    wb[:, :per2, :] = jnp.zeros((9, per2, wb.shape[2]), wb.dtype)
     pl.semaphore_wait(barrier, jnp.where(t < slabs - 1, 2 * (n - 1), n - 1) + slabs - 1)
 
     def feat_copy(source, target):
@@ -261,18 +275,13 @@
             device_id=ident(to, target), device_id_type=MESH,
         )
 
-    for delta in range(1, n):
+    for delta in reversed(range(1, n)):
         feat_copy(me, member(delta)).start()
 
     @pl.when(t < slabs - 1)
     def _():
-        for delta in range(n):
+        for delta in reversed(range(n)):
             feat_next(me, member(delta), t + 1).start()
-
-    for load in loads:
-        load.start()
-    wa[:, 3 * per2 :, :] = jnp.zeros((9, 4 * per2 - 3 * per2, wa.shape[2]), wa.dtype)
-    wb[:, :per2, :] = jnp.zeros((9, per2, wb.shape[2]), wb.dtype)
 
     lane = lane_of((8, LANES))
     lane_in = lax.broadcasted_iota(jnp.int32, (LANES, LANES), 0)
@@ -298,6 +307,8 @@
             result = jnp.where(me == d, twice, result)
         return result[0:1]
 
+    for load in params:
+        load.wait()
     g1, b1 = own_full(gain1), own_full(shift1)
     g2, b2, c1 = own_twice(gain2), own_twice(shift2), own_twice(bias1)
 
@@ -321,21 +332,12 @@
         x = xall[2 + f].reshape(area, LANES)
         scut[f] = jnp.dot(x, wsv[...], preferred_element_type=jnp.float32)
 
-    @pl.when(t > 0)
-    def _():
-        for delta in range(n):
-            feat_next(member(delta), me, t).wait_recv()
-
-    @pl.when(t == 0)
-    def _():
-        xall[0] = xall[2]
-        xall[1] = xall[2]
-
     for delta in range(1, slabs):
         stat_copy(stat1, slab(delta), t, s1s_sem, s1r_sem).wait_recv()
     mean, inv = group_stats(stat1[...], same1, size1, float(2 * area))
     scale = inv * g1
-    for f in range(4):
+
+    def normalise(f):
         x = xall[f].reshape(area, LANES).astype(jnp.float32)
         h = silu((x - mean) * scale + b1)
         left, right = side_shifts(h, width)
@@ -346,79 +348,99 @@
             xp1[f, 0, :, lanes] = part[0]
             xp1[f, height + 1, :, lanes] = part[height - 1]
 
+    depth = 9 * LANES
+    tall = height // 2
+    half = tall * width
+
+    def conv1(dt, s):
+        rows_in = [xp1[dt : dt + 2, s * tall + dy : (s + 1) * tall + dy] for dy in range(3)]
+        lhs = jnp.concatenate([x.reshape(2 * half, 3 * LANES) for x in rows_in], axis=1)
+        rhs = w1v[dt * depth : (dt + 1) * depth, :]
+        return jnp.dot(lhs, rhs, preferred_element_type=jnp.float32)
+
+    normalise(2)
+    normalise(3)
     loads[0].wait()
-    depth = 9 * LANES
-    firsts = []
-    for f in range(2):
-        total = None
-        for dt in range(3):
-            lhs = jnp.concatenate(
-                [xp1[f + dt, dy : dy + height].reshape(area, 3 * LANES) for dy in range(3)], axis=1
-            )
-            term = jnp.dot(
-                lhs, w1v[dt * depth : (dt + 1) * depth, :], preferred_element_type=jnp.float32
-            )
-            total = term if total is None else total + term
-        firsts.append(total)
-    wide = lane_of((area, LANES))
-    for d in range(n):
-        k = d // 2 * LANES
-        one, two = firsts[0][:, k : k + LANES], firsts[1][:, k : k + LANES]
-        if d % 2 == 0:
-            packed = jnp.where(wide < per2, one, pltpu.roll(two, per2, 1))
-        else:
-            packed = jnp.where(wide < per2, pltpu.roll(one, per2, 1), two)
-        part1[d] = packed
-        send1[d] = packed.astype(jnp.bfloat16)
-
-    def sum_copy(src, dst, source, target, ssem, rsem):
+    for s in range(2):
+        acc[s] = conv1(2, s)
+
+    @pl.when(t > 0)
+    def _():
+        for delta in range(n):
+            feat_next(member(delta), me, t).wait_recv()
+
+    @pl.when(t == 0)
+    def _():
+        xall[0] = xall[2]
+        xall[1] = xall[2]
+
+    normalise(0)
+    normalise(1)
+
+    def piece_copy(src, dst, source, target, s, ssem, rsem):
         return pltpu.make_async_remote_copy(
-            src_ref=src.at[target], dst_ref=dst.at[source],
-            send_sem=ssem.at[target], recv_sem=rsem.at[source],
+            src_ref=src.at[s, target], dst_ref=dst.at[s, source],
+            send_sem=ssem.at[s, target], recv_sem=rsem.at[s, source],
             device_id=ident(t, target), device_id_type=MESH,
         )
 
-    for delta in range(1, n):
-        sum_copy(send1, recv1, me, member(delta), r1s_sem, r1r_sem).start()
-    middle = part1[me] + c1
-    for delta in range(1, n):
-        source = member(delta)
-        sum_copy(send1, recv1, source, me, r1s_sem, r1r_sem).wait_recv()
-        middle = middle + recv1[source].astype(jnp.float32)
-
-    midbf[...] = middle.astype(jnp.bfloat16)
-
-    def mid_copy(to):
+    wide = lane_of((half, LANES))
+    for s in range(2):
+        total = acc[s] + conv1(1, s) + conv1(0, s)
+        for d in range(n):
+            k = d // 2 * LANES
+            one, two = total[:half, k : k + LANES], total[half:, k : k + LANES]
+            if d % 2 == 0:
+                packed = jnp.where(wide < per2, one, pltpu.roll(two, per2, 1))
+            else:
+                packed = jnp.where(wide < per2, pltpu.roll(one, per2, 1), two)
+            part1[s, d] = packed
+            send1[s, d] = packed.astype(jnp.bfloat16)
+        for delta in reversed(range(1, n)):
+            piece_copy(send1, recv1, me, member(delta), s, r1s_sem, r1r_sem).start()
+
+    def mid_copy(to, s):
         return pltpu.make_async_remote_copy(
-            src_ref=midbf, dst_ref=prevbf, send_sem=ps_sem, recv_sem=pr_sem,
+            src_ref=midbf.at[s], dst_ref=prevbf.at[s],
+            send_sem=ps_sem.at[s], recv_sem=pr_sem.at[s],
             device_id=ident(to, me), device_id_type=MESH,
         )
 
-    stat2[t] = lane_stats(middle)
+    for s in range(2):
+        middle = part1[s, me] + c1
+        for delta in range(1, n):
+            source = member(delta)
+            piece_copy(send1, recv1, source, me, s, r1s_sem, r1r_sem).wait_recv()
+            middle = middle + recv1[s, source].astype(jnp.float32)
+        midbf[s] = middle.astype(jnp.bfloat16)
+        mids[1, s] = middle
+
+        @pl.when(t < slabs - 1)
+        def _():
+            mid_copy(t + 1, s).start()
+
+    stat2[t] = lane_stats(mids[1].reshape(area, LANES))
     for delta in range(1, slabs):
         stat_copy(stat2, t, slab(delta), s2s_sem, s2r_sem).start()
 
-    @pl.when(t < slabs - 1)
-    def _():
-        mid_copy(t + 1).start()
-
-    part1[0] = middle
-
     @pl.when(t > 0)
     def _():
-        mid_copy(t).wait_recv()
-        part1[1] = prevbf[...].astype(jnp.float32)
+        for s in range(2):
+            mid_copy(t, s).wait_recv()
+            mids[0, s] = prevbf[s].astype(jnp.float32)
 
     @pl.when(t == 0)
     def _():
-        part1[1] = jnp.where(wide < per2, middle, pltpu.roll(middle, per2, 1))
+        for s in range(2):
+            middle = mids[1, s]
+            mids[0, s] = jnp.where(wide < per2, middle, pltpu.roll(middle, per2, 1))
 
     for delta in range(1, slabs):
         stat_copy(stat2, slab(delta), t, s2s_sem, s2r_sem).wait_recv()
     mean, inv = group_stats(stat2[...], same2, 2 * size2, float(area))
     scale = inv * g2
     for i in range(2):
-        h = silu((part1[1 - i] - mean) * scale + b2)
+        h = silu((mids[i].reshape(area, LANES) - mean) * scale + b2)
         left, right = side_shifts(h, width)
         for dx, part in enumerate((left, h, right)):
             part = part.astype(jnp.bfloat16).reshape(height, width, LANES)
@@ -439,23 +461,26 @@
         for d in range(n):
             ri, ci = d // ncol, d % ncol
             piece = total[ri * rows : (ri + 1) * rows, ci * cols : (ci + 1) * cols]
-            part2[d, f] = piece
-            send2[d, f] = piece.astype(jnp.bfloat16)
-
-    for delta in range(1, n):
-        sum_copy(send2, recv2, me, member(delta), r2s_sem, r2r_sem).start()
-    result = part2[me] + bias2[...].reshape(1, 1, 1, -1)
-    for delta in range(1, n):
-        source = member(delta)
-        sum_copy(send2, recv2, source, me, r2s_sem, r2r_sem).wait_recv()
-        result = result + recv2[source].astype(jnp.float32)
-    out[...] = result.astype(out.dtype)
+            part2[f, d] = piece
+            send2[f, d] = piece.astype(jnp.bfloat16)
+        for delta in reversed(range(1, n)):
+            piece_copy(send2, recv2, me, member(delta), f, r2s_sem, r2r_sem).start()
+
+    last = bias2[...].reshape(1, 1, -1)
+    for f in range(2):
+        result = part2[f, me] + last
+        for delta in range(1, n):
+            source = member(delta)
+            piece_copy(send2, recv2, source, me, f, r2s_sem, r2r_sem).wait_recv()
+            result = result + recv2[f, source].astype(jnp.float32)
+        out[f] = result.astype(out.dtype)
 
     for delta in range(1, n):
         target = member(delta)
         feat_copy(me, target).wait_send()
-        sum_copy(send1, recv1, me, target, r1s_sem, r1r_sem).wait_send()
-        sum_copy(send2, recv2, me, target, r2s_sem, r2r_sem).wait_send()
+        for s in range(2):
+            piece_copy(send1, recv1, me, target, s, r1s_sem, r1r_sem).wait_send()
+            piece_copy(send2, recv2, me, target, s, r2s_sem, r2r_sem).wait_send()
     for delta in range(1, slabs):
         stat_copy(stat1, t, slab(delta), s1s_sem, s1r_sem).wait_send()
         stat_copy(stat2, t, slab(delta), s2s_sem, s2r_sem).wait_send()
@@ -464,7 +489,8 @@
     def _():
         for delta in range(n):
             feat_next(me, member(delta), t + 1).wait_send()
-        mid_copy(t + 1).wait_send()
+        for s in range(2):
+            mid_copy(t + 1, s).wait_send()
 
 
 def per_device(
@@ -487,7 +513,7 @@
     height, width = nrow * rows, ncol * cols
     area = height * width
     fits = frames == 2 and per1 == LANES and 2 * per2 == LANES and cols % 16 == 0
-    fits = fits and width & (width - 1) == 0 and GROUPS % n == 0
+    fits = fits and width & (width - 1) == 0 and GROUPS % n == 0 and height % 2 == 0
     if not fits:
         return per_device_gathered(
             features, gn1_gain, gn1_bias, conv1_weight, conv1_bias, skip_weight,
@@ -495,7 +521,14 @@
         )
     bf16, f32 = jnp.bfloat16, jnp.float32
     vmem, dma = pltpu.VMEM, pltpu.SemaphoreType.DMA
+    half = area // 2
     scratch = [
+        vmem((1, chans_in), f32),
+        vmem((1, chans_in), f32),
+        vmem((1, chans_out), f32),
+        vmem((1, chans_out), f32),
+        vmem((1, chans_out), f32),
+        vmem((1, chans_out), f32),
         vmem((4, height, width, LANES), bf16),
         vmem((27 * per1, chans_out), bf16),
         vmem((per1, chans_out), bf16),
@@ -503,36 +536,36 @@
         vmem((9, 4 * per2, chans_out), bf16),
         vmem((4, height + 2, width, 3 * LANES), bf16),
         vmem((height + 2, width, 6 * LANES), bf16),
-        vmem((n, area, LANES), f32),
-        vmem((n, area, LANES), bf16),
-        vmem((n, area, LANES), bf16),
+        vmem((2, area, chans_out), f32),
+        vmem((2, n, half, LANES), f32),
+        vmem((2, n, half, LANES), bf16),
+        vmem((2, n, half, LANES), bf16),
         vmem((slabs, 8, LANES), f32),
         vmem((slabs, 8, LANES), f32),
-        vmem((area, LANES), bf16),
-        vmem((area, LANES), bf16),
+        vmem((2, 2, half, LANES), f32),
+        vmem((2, half, LANES), bf16),
+        vmem((2, half, LANES), bf16),
         vmem((2, area, chans_out), f32),
-        vmem((n, 2, rows, cols, chans_out), f32),
-        vmem((n, 2, rows, cols, chans_out), bf16),
-        vmem((n, 2, rows, cols, chans_out), bf16),
-        dma((8,)), dma, dma((n,)), dma((n,)), dma((n,)), dma((n,)),
+        vmem((2, n, rows, cols, chans_out), f32),
+        vmem((2, n, rows, cols, chans_out), bf16),
+        vmem((2, n, rows, cols, chans_out), bf16),
+        dma((8,)), dma((6,)), dma, dma((n,)), dma((n,)), dma((n,)), dma((n,)),
         dma((slabs,)), dma((slabs,)), dma((slabs,)), dma((slabs,)),
-        dma((n,)), dma((n,)), dma((n,)), dma((n,)),
-        dma, dma,
+        dma((2, n)), dma((2, n)), dma((2, n)), dma((2, n)),
+        dma((2,)), dma((2,)),
     ]
-    anywhere = pl.BlockSpec(memory_space=pl.ANY)
+    stays = pl.BlockSpec(memory_space=pltpu.HBM)
     inside = pl.BlockSpec(memory_space=pltpu.VMEM)
     sizes = (slabs, nrow, ncol, rows, cols, per1, per2)
     flops = 2 * 2 * area * chans_out * (28 * per1 + 27 * per2)
     return pl.pallas_call(
         functools.partial(block_kernel, sizes),
         out_shape=jax.ShapeDtypeStruct((frames, rows, cols, chans_out), bf16),
-        in_specs=[
-            anywhere, inside, inside, anywhere, inside, anywhere, inside, inside, anywhere, inside,
-        ],
+        in_specs=[stays] * 10,
         out_specs=inside,
         scratch_shapes=scratch,
         compiler_params=pltpu.CompilerParams(
-            collective_id=0, has_side_effects=True, vmem_limit_bytes=48 * 1024 * 1024
+            collective_id=0, has_side_effects=True, vmem_limit_bytes=64 * 1024 * 1024
         ),
         cost_estimate=pl.CostEstimate(
             flops=flops, bytes_accessed=4 * 1024 * 1024, transcendentals=6 * area * LANES

time: 43.7 us -> 37 us (0.85)
  the two profiles are of different devices: /device:TPU:1 before, /device:TPU:0 now
where the time goes in v2:
time: 37 us; the launch traced here: 36.8 us
  Pallas kernels  35.3 us (95%)
  local copies, waits for them, and re-layouts  1.54 us (4%)
    pallas_call x1, Pallas kernels, per_device(): pl.pallas_call(functools.partial(block_kernel, sizes), out_shape=jax.Shap...  35.3 us
    unnamed x1, local copies, waits for them, and re-layouts  1.54 us

profile of v2, /device:TPU:0, one launch (start us, length us, event | category | flops | bytes accessed | tf_op | source)
XLA Modules:
  0.0 36.8 jit_solution(5681925604083572005)
XLA Ops:
  0.0 35.3 %residual_block.1 = bf16[2,6,16,256]{3,2,1,0:T(8,128)(2,1)} custom-call(bf16[2,6,16,512]{3,2,1,0:T(8,128)(2,1)} %feat.1, f32[1,512]{1,0:T(1,128)} %bitcast.12, f32[1,512]{1,0:T(1,128)} %bitcast.13, bf16[3456,256]{1,0:T(8,128)(2,1)} %bitcast.9, f32[1,256]{1,0:T(1,128)} %bitcast.14, bf16[128,256]{1,0:T(8,128)(2,1)} %bitcast.11, f32[1,256]{1,0:T(1,128)} %bitcast.15, ...), custom_call_target="tpu_custom_call" | custom-call | flops 2088763392 | bytes 4194304 | tf_op jit(solution)/shard_map/residual_block/pallas_call | solution.py:561
  35.3 1.5 %copy.12 = bf16[2,6,16,256]{3,2,1,0:T(8,128)(2,1)} copy(bf16[2,6,16,256]{3,2,1,0:T(8,128)(2,1)} %residual_block.1) | data formatting | bytes 196608

commit v3 on v2

--- a/solution.py
+++ b/solution.py
@@ -147,21 +147,20 @@
     return jnp.where(row == 0, mean, jnp.where(row == 1, spread, 0.0))
 
 
-def group_stats(stats, same, lanes, count):
-    devices = stats.shape[0]
-    means, spreads = stats[:, 0:1, :], stats[:, 1:2, :]
-    mean = jnp.sum(means, axis=0) * (1.0 / devices)
+def group_stats(means, spreads, same, lanes, count):
+    parts = means.shape[0]
+    mean = jnp.sum(means, axis=0) * (1.0 / parts)
     spread = jnp.sum(spreads, axis=0) + count * jnp.sum((means - mean[None]) ** 2, axis=0)
     mean = jnp.broadcast_to(mean, (8, LANES))
     group_mean = (
         jnp.dot(mean, same, precision=lax.Precision.HIGHEST, preferred_element_type=jnp.float32)
         * (1.0 / lanes)
     )
-    spread = spread + (count * devices) * (mean - group_mean) ** 2
+    spread = spread + (count * parts) * (mean - group_mean) ** 2
     total = jnp.dot(
         spread, same, precision=lax.Precision.HIGHEST, preferred_element_type=jnp.float32
     )
-    inv = lax.rsqrt(total * (1.0 / (count * devices * lanes)) + 1e-6)
+    inv = lax.rsqrt(total * (1.0 / (count * parts * lanes)) + 1e-6)
     return group_mean[0:1], inv[0:1]
 
 
@@ -177,10 +176,12 @@
     sizes,
     feat, gain1_hbm, shift1_hbm, w1, bias1_hbm, wskip, gain2_hbm, shift2_hbm, w2, bias2_hbm,
     out,
-    gain1, shift1, bias1, gain2, shift2, bias2, xall, w1v, wsv, wa, wb, xp1, xp2, acc, part1, send1, recv1, stat1, stat2,
-    mids, midbf, prevbf, scut, part2, send2, recv2,
+    gain1, shift1, bias1, gain2, shift2, bias2, featv, xall, w1v, wsv, wcat, xp1, xp2,
+    acc, part1, send1, recv1, sum1, send1b, recv1b, stat0, statg, stat2,
+    mids, midbf, prevbf, scut, part2, send2, recv2, sum2, send2b, recv2b,
     w_sem, p_sem, own_sem, fs_sem, fr_sem, fps_sem, fpr_sem,
-    s1s_sem, s1r_sem, s2s_sem, s2r_sem, r1s_sem, r1r_sem, r2s_sem, r2r_sem,
+    s1s_sem, s1r_sem, sgs_sem, sgr_sem, s2s_sem, s2r_sem,
+    r1s_sem, r1r_sem, r1bs_sem, r1br_sem, r2s_sem, r2r_sem, r2bs_sem, r2br_sem,
     ps_sem, pr_sem,
 ):
     slabs, nrow, ncol, rows, cols, per1, per2 = sizes
@@ -209,17 +210,15 @@
         pltpu.make_async_copy(w1, w1v, w_sem.at[0]),
         pltpu.make_async_copy(wskip, wsv, w_sem.at[1]),
     ]
-    for dt in range(3):
-        lo = dt * per2
-        loads.append(
-            pltpu.make_async_copy(w2.at[dt], wa.at[:, lo : lo + per2, :], w_sem.at[2 + dt])
-        )
+    for i, (f, p, place_in, dt) in enumerate(
+        ((0, 0, 0, 0), (0, 0, 1, 1), (0, 1, 0, 2), (1, 0, 1, 0), (1, 1, 0, 1), (1, 1, 1, 2))
+    ):
+        lo = place_in * per2
         loads.append(
             pltpu.make_async_copy(
-                w2.at[dt], wb.at[:, lo + per2 : lo + 2 * per2, :], w_sem.at[5 + dt]
+                w2.at[dt], wcat.at[f, p, :, lo : lo + per2, :], w_sem.at[2 + i]
             )
         )
-
     params = [
         pltpu.make_async_copy(source, target, p_sem.at[i])
         for i, (source, target) in enumerate(
@@ -239,7 +238,9 @@
     def chunk(i):
         return feat.at[:, :, :, pl.ds(pl.multiple_of(i * LANES, LANES), LANES)]
 
-    own = pltpu.make_async_copy(chunk(me), window(2, me), own_sem)
+    whole = pltpu.make_async_copy(feat, featv, own_sem.at[1])
+    whole.start()
+    own = pltpu.make_async_copy(chunk(me), window(2, me), own_sem.at[0])
     own.start()
 
     barrier = pltpu.get_barrier_semaphore()
@@ -257,9 +258,41 @@
 
     for load in params + loads:
         load.start()
-    wa[:, 3 * per2 :, :] = jnp.zeros((9, 4 * per2 - 3 * per2, wa.shape[2]), wa.dtype)
-    wb[:, :per2, :] = jnp.zeros((9, per2, wb.shape[2]), wb.dtype)
+    blank = jnp.zeros((9, per2, wcat.shape[4]), wcat.dtype)
+    wcat[0, 1, :, per2:, :] = blank
+    wcat[1, 0, :, :per2, :] = blank
+
+    row8 = lax.broadcasted_iota(jnp.int32, (2 * n, LANES), 0)
+    spots = float(2 * rows * cols)
+    whole.wait()
+    x = featv[...].reshape(2 * rows * cols, n * LANES).astype(jnp.float32)
+    lane_mean = jnp.sum(x, axis=0, keepdims=True) * (1.0 / spots)
+    lane_spread = jnp.sum((x - lane_mean) ** 2, axis=0, keepdims=True)
+    tile = jnp.zeros((2 * n, LANES), jnp.float32)
+    for d in range(n):
+        at = slice(d * LANES, (d + 1) * LANES)
+        tile = jnp.where(row8 == d, lane_mean[:, at], tile)
+        tile = jnp.where(row8 == n + d, lane_spread[:, at], tile)
+    stat0[t] = tile
+
     pl.semaphore_wait(barrier, jnp.where(t < slabs - 1, 2 * (n - 1), n - 1) + slabs - 1)
+
+    def stat_copy(buf, source, target, ssem, rsem):
+        return pltpu.make_async_remote_copy(
+            src_ref=buf.at[source], dst_ref=buf.at[source],
+            send_sem=ssem.at[target], recv_sem=rsem.at[source],
+            device_id=ident(target, me), device_id_type=MESH,
+        )
+
+    def share_copy(source, target):
+        return pltpu.make_async_remote_copy(
+            src_ref=statg.at[source], dst_ref=statg.at[source],
+            send_sem=sgs_sem.at[target], recv_sem=sgr_sem.at[source],
+            device_id=ident(t, target), device_id_type=MESH,
+        )
+
+    for delta in reversed(range(1, slabs)):
+        stat_copy(stat0, t, slab(delta), s1s_sem, s1r_sem).start()
 
     def feat_copy(source, target):
         return pltpu.make_async_remote_copy(
@@ -312,29 +345,31 @@
     g1, b1 = own_full(gain1), own_full(shift1)
     g2, b2, c1 = own_twice(gain2), own_twice(shift2), own_twice(bias1)
 
-    def stat_copy(buf, source, target, ssem, rsem):
-        return pltpu.make_async_remote_copy(
-            src_ref=buf.at[source], dst_ref=buf.at[source],
-            send_sem=ssem.at[target], recv_sem=rsem.at[source],
-            device_id=ident(target, me), device_id_type=MESH,
-        )
+    for delta in range(1, slabs):
+        stat_copy(stat0, slab(delta), t, s1s_sem, s1r_sem).wait_recv()
+    stats = stat0[...]
+    total = jnp.sum(stats, axis=0)
+    mean = total * (1.0 / slabs)
+    off = spots * jnp.sum((stats - mean[None]) ** 2, axis=0)
+    statg[me] = jnp.where(row8 < n, mean, total + pltpu.roll(off, n, 0))
+    for delta in reversed(range(1, n)):
+        share_copy(me, member(delta)).start()
 
     own.wait()
     for delta in range(1, n):
         feat_copy(member(delta), me).wait_recv()
-    raw = xall[2:4].reshape(2 * area, LANES).astype(jnp.float32)
-    stat1[t] = lane_stats(raw)
-    for delta in range(1, slabs):
-        stat_copy(stat1, t, slab(delta), s1s_sem, s1r_sem).start()
-
     loads[1].wait()
     for f in range(2):
         x = xall[2 + f].reshape(area, LANES)
         scut[f] = jnp.dot(x, wsv[...], preferred_element_type=jnp.float32)
 
-    for delta in range(1, slabs):
-        stat_copy(stat1, slab(delta), t, s1s_sem, s1r_sem).wait_recv()
-    mean, inv = group_stats(stat1[...], same1, size1, float(2 * area))
+    for delta in range(1, n):
+        share_copy(member(delta), me).wait_recv()
+    stats = statg[...]
+    pick = lax.broadcasted_iota(jnp.int32, stats.shape, 1)
+    means = jnp.sum(jnp.where(pick == me, stats, 0.0), axis=1, keepdims=True)
+    spreads = jnp.sum(jnp.where(pick == n + me, stats, 0.0), axis=1, keepdims=True)
+    mean, inv = group_stats(means, spreads, same1, size1, spots * slabs)
     scale = inv * g1
 
     def normalise(f):
@@ -377,12 +412,52 @@
     normalise(0)
     normalise(1)
 
-    def piece_copy(src, dst, source, target, s, ssem, rsem):
+    def core_copy(src, dst, source, target, s, ssem, rsem):
         return pltpu.make_async_remote_copy(
             src_ref=src.at[s, target], dst_ref=dst.at[s, source],
             send_sem=ssem.at[s, target], recv_sem=rsem.at[s, source],
-            device_id=ident(t, target), device_id_type=MESH,
-        )
+            device_id={"tm": t, "row": r, "col": target}, device_id_type=MESH,
+        )
+
+    def row_copy(src, dst, source, target, s, ssem, rsem):
+        return pltpu.make_async_remote_copy(
+            src_ref=src.at[s, target], dst_ref=dst.at[s, source],
+            send_sem=ssem.at[s, target], recv_sem=rsem.at[s, source],
+            device_id={"tm": t, "row": target, "col": c}, device_id_type=MESH,
+        )
+
+    cores = [lax.rem(c + delta, ncol) for delta in range(1, ncol)]
+    others = [lax.rem(r + delta, nrow) for delta in range(1, nrow)]
+
+    def to_cores(stage, s):
+        send, recv, ssem, rsem = stage
+        for core in cores:
+            core_copy(send, recv, c, core, s, ssem, rsem).start()
+
+    def to_rows(stage, part, total, stage_b, s):
+        send, recv, ssem, rsem = stage
+        send_b, recv_b, ssem_b, rsem_b = stage_b
+        summed = part[s, c]
+        for core in cores:
+            core_copy(send, recv, core, c, s, ssem, rsem).wait_recv()
+            summed = summed + recv[s, core].astype(jnp.float32)
+        total[s] = summed
+        send_b[s] = summed.astype(jnp.bfloat16)
+        for other in others:
+            row_copy(send_b, recv_b, r, other, s, ssem_b, rsem_b).start()
+
+    def from_rows(total, stage_b, s):
+        send_b, recv_b, ssem_b, rsem_b = stage_b
+        result = total[s, r]
+        for other in others:
+            row_copy(send_b, recv_b, other, r, s, ssem_b, rsem_b).wait_recv()
+            result = result + recv_b[s, other].astype(jnp.float32)
+        return result
+
+    first = (send1, recv1, r1s_sem, r1r_sem)
+    first_b = (send1b, recv1b, r1bs_sem, r1br_sem)
+    second = (send2, recv2, r2s_sem, r2r_sem)
+    second_b = (send2b, recv2b, r2bs_sem, r2br_sem)
 
     wide = lane_of((half, LANES))
     for s in range(2):
@@ -394,10 +469,11 @@
                 packed = jnp.where(wide < per2, one, pltpu.roll(two, per2, 1))
             else:
                 packed = jnp.where(wide < per2, pltpu.roll(one, per2, 1), two)
-            part1[s, d] = packed
-            send1[s, d] = packed.astype(jnp.bfloat16)
-        for delta in reversed(range(1, n)):
-            piece_copy(send1, recv1, me, member(delta), s, r1s_sem, r1r_sem).start()
+            part1[s, d % ncol, d // ncol] = packed
+            send1[s, d % ncol, d // ncol] = packed.astype(jnp.bfloat16)
+        to_cores(first, s)
+    for s in range(2):
+        to_rows(first, part1, sum1, first_b, s)
 
     def mid_copy(to, s):
         return pltpu.make_async_remote_copy(
@@ -406,22 +482,51 @@
             device_id=ident(to, me), device_id_type=MESH,
         )
 
-    for s in range(2):
-        middle = part1[s, me] + c1
-        for delta in range(1, n):
-            source = member(delta)
-            piece_copy(send1, recv1, source, me, s, r1s_sem, r1r_sem).wait_recv()
-            middle = middle + recv1[s, source].astype(jnp.float32)
-        midbf[s] = middle.astype(jnp.bfloat16)
-        mids[1, s] = middle
-
+    def pass_on(s):
         @pl.when(t < slabs - 1)
         def _():
             mid_copy(t + 1, s).start()
 
+    for s in range(2):
+        middle = from_rows(sum1, first_b, s) + c1
+        midbf[s] = middle.astype(jnp.bfloat16)
+        mids[1, s] = middle
+        if s == 0:
+            pass_on(0)
+
     stat2[t] = lane_stats(mids[1].reshape(area, LANES))
+    for delta in reversed(range(1, slabs)):
+        stat_copy(stat2, t, slab(delta), s2s_sem, s2r_sem).start()
+    pass_on(1)
+
     for delta in range(1, slabs):
-        stat_copy(stat2, t, slab(delta), s2s_sem, s2r_sem).start()
+        stat_copy(stat2, slab(delta), t, s2s_sem, s2r_sem).wait_recv()
+    stats = stat2[...]
+    mean, inv = group_stats(stats[:, 0:1], stats[:, 1:2], same2, 2 * size2, float(area))
+    scale = inv * g2
+
+    def normalise_mid(i):
+        h = silu((mids[i].reshape(area, LANES) - mean) * scale + b2)
+        left, right = side_shifts(h, width)
+        for dx, part in enumerate((left, h, right)):
+            part = part.astype(jnp.bfloat16).reshape(height, width, LANES)
+            lanes = slice(dx * LANES, (dx + 1) * LANES)
+            xp2[i, 1 : height + 1, :, lanes] = part
+            xp2[i, 0, :, lanes] = part[0]
+            xp2[i, height + 1, :, lanes] = part[height - 1]
+
+    def conv2(f, i):
+        rows_in = [xp2[i, dy : dy + height].reshape(area, 3 * LANES) for dy in range(3)]
+        rhs = wcat[f, i].reshape(9 * LANES, wcat.shape[4])
+        return jnp.dot(
+            jnp.concatenate(rows_in, axis=1), rhs, preferred_element_type=jnp.float32
+        )
+
+    normalise_mid(1)
+    for load in loads[2:]:
+        load.wait()
+    for f in range(2):
+        scut[f] = scut[f] + conv2(f, 1)
 
     @pl.when(t > 0)
     def _():
@@ -435,54 +540,33 @@
             middle = mids[1, s]
             mids[0, s] = jnp.where(wide < per2, middle, pltpu.roll(middle, per2, 1))
 
-    for delta in range(1, slabs):
-        stat_copy(stat2, slab(delta), t, s2s_sem, s2r_sem).wait_recv()
-    mean, inv = group_stats(stat2[...], same2, 2 * size2, float(area))
-    scale = inv * g2
-    for i in range(2):
-        h = silu((mids[i].reshape(area, LANES) - mean) * scale + b2)
-        left, right = side_shifts(h, width)
-        for dx, part in enumerate((left, h, right)):
-            part = part.astype(jnp.bfloat16).reshape(height, width, LANES)
-            lanes = slice((2 * dx + i) * LANES, (2 * dx + i + 1) * LANES)
-            xp2[1 : height + 1, :, lanes] = part
-            xp2[0, :, lanes] = part[0]
-            xp2[height + 1, :, lanes] = part[height - 1]
-
-    for load in loads[2:]:
-        load.wait()
-    for f, weight in enumerate((wa, wb)):
-        total = scut[f]
-        for dy in range(3):
-            lhs = xp2[dy : dy + height].reshape(area, 6 * LANES)
-            rhs = weight[3 * dy : 3 * dy + 3].reshape(6 * LANES, weight.shape[2])
-            total = total + jnp.dot(lhs, rhs, preferred_element_type=jnp.float32)
-        total = total.reshape(height, width, weight.shape[2])
-        for d in range(n):
-            ri, ci = d // ncol, d % ncol
-            piece = total[ri * rows : (ri + 1) * rows, ci * cols : (ci + 1) * cols]
-            part2[f, d] = piece
-            send2[f, d] = piece.astype(jnp.bfloat16)
-        for delta in reversed(range(1, n)):
-            piece_copy(send2, recv2, me, member(delta), f, r2s_sem, r2r_sem).start()
-
+    normalise_mid(0)
+    for f in range(2):
+        total = (scut[f] + conv2(f, 0)).reshape(nrow, rows, width, wcat.shape[4])
+        for ci in range(ncol):
+            piece = total[:, :, ci * cols : (ci + 1) * cols]
+            part2[f, ci] = piece
+            send2[f, ci] = piece.astype(jnp.bfloat16)
+        to_cores(second, f)
+    for f in range(2):
+        to_rows(second, part2, sum2, second_b, f)
     last = bias2[...].reshape(1, 1, -1)
     for f in range(2):
-        result = part2[f, me] + last
-        for delta in range(1, n):
-            source = member(delta)
-            piece_copy(send2, recv2, source, me, f, r2s_sem, r2r_sem).wait_recv()
-            result = result + recv2[f, source].astype(jnp.float32)
-        out[f] = result.astype(out.dtype)
+        out[f] = (from_rows(sum2, second_b, f) + last).astype(out.dtype)
 
     for delta in range(1, n):
         target = member(delta)
         feat_copy(me, target).wait_send()
-        for s in range(2):
-            piece_copy(send1, recv1, me, target, s, r1s_sem, r1r_sem).wait_send()
-            piece_copy(send2, recv2, me, target, s, r2s_sem, r2r_sem).wait_send()
+        share_copy(me, target).wait_send()
+    for s in range(2):
+        for send, recv, ssem, rsem in (first, second):
+            for core in cores:
+                core_copy(send, recv, c, core, s, ssem, rsem).wait_send()
+        for send, recv, ssem, rsem in (first_b, second_b):
+            for other in others:
+                row_copy(send, recv, r, other, s, ssem, rsem).wait_send()
     for delta in range(1, slabs):
-        stat_copy(stat1, t, slab(delta), s1s_sem, s1r_sem).wait_send()
+        stat_copy(stat0, t, slab(delta), s1s_sem, s1r_sem).wait_send()
         stat_copy(stat2, t, slab(delta), s2s_sem, s2r_sem).wait_send()
 
     @pl.when(t < slabs - 1)
@@ -513,7 +597,7 @@
     height, width = nrow * rows, ncol * cols
     area = height * width
     fits = frames == 2 and per1 == LANES and 2 * per2 == LANES and cols % 16 == 0
-    fits = fits and width & (width - 1) == 0 and GROUPS % n == 0 and height % 2 == 0
+    fits = fits and n == 4 and width & (width - 1) == 0 and GROUPS % n == 0 and height % 2 == 0
     if not fits:
         return per_device_gathered(
             features, gn1_gain, gn1_bias, conv1_weight, conv1_bias, skip_weight,
@@ -529,29 +613,37 @@
         vmem((1, chans_out), f32),
         vmem((1, chans_out), f32),
         vmem((1, chans_out), f32),
+        vmem((frames, rows, cols, chans_in), bf16),
         vmem((4, height, width, LANES), bf16),
         vmem((27 * per1, chans_out), bf16),
         vmem((per1, chans_out), bf16),
-        vmem((9, 4 * per2, chans_out), bf16),
-        vmem((9, 4 * per2, chans_out), bf16),
+        vmem((2, 2, 9, 2 * per2, chans_out), bf16),
         vmem((4, height + 2, width, 3 * LANES), bf16),
-        vmem((height + 2, width, 6 * LANES), bf16),
+        vmem((2, height + 2, width, 3 * LANES), bf16),
         vmem((2, area, chans_out), f32),
-        vmem((2, n, half, LANES), f32),
-        vmem((2, n, half, LANES), bf16),
-        vmem((2, n, half, LANES), bf16),
-        vmem((slabs, 8, LANES), f32),
+        vmem((2, ncol, nrow, half, LANES), f32),
+        vmem((2, ncol, nrow, half, LANES), bf16),
+        vmem((2, ncol, nrow, half, LANES), bf16),
+        vmem((2, nrow, half, LANES), f32),
+        vmem((2, nrow, half, LANES), bf16),
+        vmem((2, nrow, half, LANES), bf16),
+        vmem((slabs, 2 * n, LANES), f32),
+        vmem((n, 2 * n, LANES), f32),
         vmem((slabs, 8, LANES), f32),
         vmem((2, 2, half, LANES), f32),
         vmem((2, half, LANES), bf16),
         vmem((2, half, LANES), bf16),
         vmem((2, area, chans_out), f32),
-        vmem((2, n, rows, cols, chans_out), f32),
-        vmem((2, n, rows, cols, chans_out), bf16),
-        vmem((2, n, rows, cols, chans_out), bf16),
-        dma((8,)), dma((6,)), dma, dma((n,)), dma((n,)), dma((n,)), dma((n,)),
-        dma((slabs,)), dma((slabs,)), dma((slabs,)), dma((slabs,)),
-        dma((2, n)), dma((2, n)), dma((2, n)), dma((2, n)),
+        vmem((2, ncol, nrow, rows, cols, chans_out), f32),
+        vmem((2, ncol, nrow, rows, cols, chans_out), bf16),
+        vmem((2, ncol, nrow, rows, cols, chans_out), bf16),
+        vmem((2, nrow, rows, cols, chans_out), f32),
+        vmem((2, nrow, rows, cols, chans_out), bf16),
+        vmem((2, nrow, rows, cols, chans_out), bf16),
+        dma((8,)), dma((6,)), dma((2,)), dma((n,)), dma((n,)), dma((n,)), dma((n,)),
+        dma((slabs,)), dma((slabs,)), dma((n,)), dma((n,)), dma((slabs,)), dma((slabs,)),
+        dma((2, ncol)), dma((2, ncol)), dma((2, nrow)), dma((2, nrow)),
+        dma((2, ncol)), dma((2, ncol)), dma((2, nrow)), dma((2, nrow)),
         dma((2,)), dma((2,)),
     ]
     stays = pl.BlockSpec(memory_space=pltpu.HBM)

time: 37 us -> 36 us (0.973)
  Pallas kernels: 35.3 us -> 34.3 us
    pallas_call x1, Pallas kernels: 35.3 us -> 34.3 us  [per_device(): pl.pallas_call(functools.partial(block_kernel, sizes), out_shape=jax.Shap...]
where the time goes in v3:
time: 36 us; the launch traced here: 35.8 us
  Pallas kernels  34.3 us (95%)
  local copies, waits for them, and re-layouts  1.54 us (4%)
    pallas_call x1, Pallas kernels, per_device(): pl.pallas_call(functools.partial(block_kernel, sizes), out_shape=jax.Shap...  34.3 us
    unnamed x1, local copies, waits for them, and re-layouts  1.54 us

profile of v3, /device:TPU:0, one launch (start us, length us, event | category | flops | bytes accessed | tf_op | source)
XLA Modules:
  0.0 35.8 jit_solution(15532367428003656702)
XLA Ops:
  0.0 34.3 %residual_block.1 = bf16[2,6,16,256]{3,2,1,0:T(8,128)(2,1)} custom-call(bf16[2,6,16,512]{3,2,1,0:T(8,128)(2,1)} %feat.1, f32[1,512]{1,0:T(1,128)} %bitcast.12, f32[1,512]{1,0:T(1,128)} %bitcast.13, bf16[3456,256]{1,0:T(8,128)(2,1)} %bitcast.9, f32[1,256]{1,0:T(1,128)} %bitcast.14, bf16[128,256]{1,0:T(8,128)(2,1)} %bitcast.11, f32[1,256]{1,0:T(1,128)} %bitcast.15, ...), custom_call_target="tpu_custom_call" | custom-call | flops 2088763392 | bytes 4194304 | tf_op jit(solution)/shard_map/residual_block/pallas_call | solution.py:653
  34.3 1.5 %copy.12 = bf16[2,6,16,256]{3,2,1,0:T(8,128)(2,1)} copy(bf16[2,6,16,256]{3,2,1,0:T(8,128)(2,1)} %residual_block.1) | data formatting | bytes 196608

commit v4 on v3

--- a/solution.py
+++ b/solution.py
@@ -177,7 +177,7 @@
     feat, gain1_hbm, shift1_hbm, w1, bias1_hbm, wskip, gain2_hbm, shift2_hbm, w2, bias2_hbm,
     out,
     gain1, shift1, bias1, gain2, shift2, bias2, featv, xall, w1v, wsv, wcat, xp1, xp2,
-    acc, part1, send1, recv1, sum1, send1b, recv1b, stat0, statg, stat2,
+    acc, part1, send1, recv1, sum1, send1b, recv1b, stat0, other0, statg, stat2,
     mids, midbf, prevbf, scut, part2, send2, recv2, sum2, send2b, recv2b,
     w_sem, p_sem, own_sem, fs_sem, fr_sem, fps_sem, fpr_sem,
     s1s_sem, s1r_sem, sgs_sem, sgr_sem, s2s_sem, s2r_sem,
@@ -206,6 +206,11 @@
     def slab(delta):
         return lax.rem(t + delta, slabs)
 
+    bits = [1 << k for k in range(slabs.bit_length() - 1)]
+
+    def across(bit):
+        return t + bit - 2 * bit * lax.rem(lax.div(t, bit), 2)
+
     loads = [
         pltpu.make_async_copy(w1, w1v, w_sem.at[0]),
         pltpu.make_async_copy(wskip, wsv, w_sem.at[1]),
@@ -246,12 +251,12 @@
     barrier = pltpu.get_barrier_semaphore()
     for delta in range(1, n):
         pl.semaphore_signal(barrier, inc=1, device_id=ident(t, member(delta)), device_id_type=MESH)
-    for delta in range(1, slabs):
-        pl.semaphore_signal(barrier, inc=1, device_id=ident(slab(delta), me), device_id_type=MESH)
+    for bit in bits:
+        pl.semaphore_signal(barrier, inc=1, device_id=ident(across(bit), me), device_id_type=MESH)
 
     @pl.when(t > 0)
     def _():
-        for delta in range(1, n):
+        for delta in range(n):
             pl.semaphore_signal(
                 barrier, inc=1, device_id=ident(t - 1, member(delta)), device_id_type=MESH
             )
@@ -273,9 +278,9 @@
         at = slice(d * LANES, (d + 1) * LANES)
         tile = jnp.where(row8 == d, lane_mean[:, at], tile)
         tile = jnp.where(row8 == n + d, lane_spread[:, at], tile)
-    stat0[t] = tile
-
-    pl.semaphore_wait(barrier, jnp.where(t < slabs - 1, 2 * (n - 1), n - 1) + slabs - 1)
+    stat0[0] = tile
+
+    pl.semaphore_wait(barrier, jnp.where(t < slabs - 1, 2 * n - 1, n - 1) + len(bits))
 
     def stat_copy(buf, source, target, ssem, rsem):
         return pltpu.make_async_remote_copy(
@@ -291,8 +296,26 @@
             device_id=ident(t, target), device_id_type=MESH,
         )
 
-    for delta in reversed(range(1, slabs)):
-        stat_copy(stat0, t, slab(delta), s1s_sem, s1r_sem).start()
+    def swap_copy(k):
+        return pltpu.make_async_remote_copy(
+            src_ref=stat0.at[k], dst_ref=other0.at[k],
+            send_sem=s1s_sem.at[k], recv_sem=s1r_sem.at[k],
+            device_id=ident(across(bits[k]), me), device_id_type=MESH,
+        )
+
+    def swap(k):
+        swap_copy(k).wait_recv()
+        mine, theirs = stat0[k], other0[k]
+        off = (mine - theirs) ** 2 * (spots * bits[k] * 0.5)
+        total = mine + theirs
+        joined = jnp.where(row8 < n, 0.5 * total, total + pltpu.roll(off, n, 0))
+        if k + 1 < len(bits):
+            stat0[k + 1] = joined
+            swap_copy(k + 1).start()
+        else:
+            statg[me] = joined
+
+    swap_copy(0).start()
 
     def feat_copy(source, target):
         return pltpu.make_async_remote_copy(
@@ -310,6 +333,8 @@
 
     for delta in reversed(range(1, n)):
         feat_copy(me, member(delta)).start()
+
+    swap(0)
 
     @pl.when(t < slabs - 1)
     def _():
@@ -345,13 +370,8 @@
     g1, b1 = own_full(gain1), own_full(shift1)
     g2, b2, c1 = own_twice(gain2), own_twice(shift2), own_twice(bias1)
 
-    for delta in range(1, slabs):
-        stat_copy(stat0, slab(delta), t, s1s_sem, s1r_sem).wait_recv()
-    stats = stat0[...]
-    total = jnp.sum(stats, axis=0)
-    mean = total * (1.0 / slabs)
-    off = spots * jnp.sum((stats - mean[None]) ** 2, axis=0)
-    statg[me] = jnp.where(row8 < n, mean, total + pltpu.roll(off, n, 0))
+    for k in range(1, len(bits)):
+        swap(k)
     for delta in reversed(range(1, n)):
         share_copy(me, member(delta)).start()
 
@@ -453,6 +473,18 @@
             row_copy(send_b, recv_b, other, r, s, ssem_b, rsem_b).wait_recv()
             result = result + recv_b[s, other].astype(jnp.float32)
         return result
+
+    def sent_to_cores(stage):
+        send, recv, ssem, rsem = stage
+        for s in range(2):
+            for core in cores:
+                core_copy(send, recv, c, core, s, ssem, rsem).wait_send()
+
+    def sent_to_rows(stage):
+        send, recv, ssem, rsem = stage
+        for s in range(2):
+            for other in others:
+                row_copy(send, recv, r, other, s, ssem, rsem).wait_send()
 
     first = (send1, recv1, r1s_sem, r1r_sem)
     first_b = (send1b, recv1b, r1bs_sem, r1br_sem)
@@ -475,6 +507,17 @@
     for s in range(2):
         to_rows(first, part1, sum1, first_b, s)
 
+    for delta in range(1, n):
+        feat_copy(me, member(delta)).wait_send()
+        share_copy(me, member(delta)).wait_send()
+    for k in range(len(bits)):
+        swap_copy(k).wait_send()
+
+    @pl.when(t < slabs - 1)
+    def _():
+        for delta in range(n):
+            feat_next(me, member(delta), t + 1).wait_send()
+
     def mid_copy(to, s):
         return pltpu.make_async_remote_copy(
             src_ref=midbf.at[s], dst_ref=prevbf.at[s],
@@ -501,6 +544,8 @@
 
     for delta in range(1, slabs):
         stat_copy(stat2, slab(delta), t, s2s_sem, s2r_sem).wait_recv()
+    sent_to_cores(first)
+    sent_to_rows(first_b)
     stats = stat2[...]
     mean, inv = group_stats(stats[:, 0:1], stats[:, 1:2], same2, 2 * size2, float(area))
     scale = inv * g2
@@ -550,31 +595,20 @@
         to_cores(second, f)
     for f in range(2):
         to_rows(second, part2, sum2, second_b, f)
+    for delta in range(1, slabs):
+        stat_copy(stat2, t, slab(delta), s2s_sem, s2r_sem).wait_send()
+
+    @pl.when(t < slabs - 1)
+    def _():
+        for s in range(2):
+            mid_copy(t + 1, s).wait_send()
+
+    sent_to_cores(second)
     last = bias2[...].reshape(1, 1, -1)
     for f in range(2):
         out[f] = (from_rows(sum2, second_b, f) + last).astype(out.dtype)
 
-    for delta in range(1, n):
-        target = member(delta)
-        feat_copy(me, target).wait_send()
-        share_copy(me, target).wait_send()
-    for s in range(2):
-        for send, recv, ssem, rsem in (first, second):
-            for core in cores:
-                core_copy(send, recv, c, core, s, ssem, rsem).wait_send()
-        for send, recv, ssem, rsem in (first_b, second_b):
-            for other in others:
-                row_copy(send, recv, r, other, s, ssem, rsem).wait_send()
-    for delta in range(1, slabs):
-        stat_copy(stat0, t, slab(delta), s1s_sem, s1r_sem).wait_send()
-        stat_copy(stat2, t, slab(delta), s2s_sem, s2r_sem).wait_send()
-
-    @pl.when(t < slabs - 1)
-    def _():
-        for delta in range(n):
-            feat_next(me, member(delta), t + 1).wait_send()
-        for s in range(2):
-            mid_copy(t + 1, s).wait_send()
+    sent_to_rows(second_b)
 
 
 def per_device(
@@ -597,7 +631,7 @@
     height, width = nrow * rows, ncol * cols
     area = height * width
     fits = frames == 2 and per1 == LANES and 2 * per2 == LANES and cols % 16 == 0
-    fits = fits and n == 4 and width & (width - 1) == 0 and GROUPS % n == 0 and height % 2 == 0
+    fits = fits and n == 4 and slabs & (slabs - 1) == 0 and width & (width - 1) == 0 and GROUPS % n == 0 and height % 2 == 0
     if not fits:
         return per_device_gathered(
             features, gn1_gain, gn1_bias, conv1_weight, conv1_bias, skip_weight,
@@ -627,6 +661,7 @@
         vmem((2, nrow, half, LANES), f32),
         vmem((2, nrow, half, LANES), bf16),
         vmem((2, nrow, half, LANES), bf16),
+        vmem((slabs, 2 * n, LANES), f32),
         vmem((slabs, 2 * n, LANES), f32),
         vmem((n, 2 * n, LANES), f32),
         vmem((slabs, 8, LANES), f32),

time: 36 us -> 38.6 us (1.072)
  Pallas kernels: 34.3 us -> 37 us
    pallas_call x1, Pallas kernels: 34.3 us -> 37 us  [per_device(): pl.pallas_call(functools.partial(block_kernel, sizes), out_shape=jax.Shap...]
where the time goes in v4:
time: 38.6 us; the launch traced here: 38.5 us
  Pallas kernels  37 us (96%)
  local copies, waits for them, and re-layouts  1.54 us (4%)
    pallas_call x1, Pallas kernels, per_device(): pl.pallas_call(functools.partial(block_kernel, sizes), out_shape=jax.Shap...  37 us
    unnamed x1, local copies, waits for them, and re-layouts  1.54 us

profile of v4, /device:TPU:0, one launch (start us, length us, event | category | flops | bytes accessed | tf_op | source)
XLA Modules:
  0.0 38.5 jit_solution(13629000593558356979)
XLA Ops:
  0.0 37.0 %residual_block.1 = bf16[2,6,16,256]{3,2,1,0:T(8,128)(2,1)} custom-call(bf16[2,6,16,512]{3,2,1,0:T(8,128)(2,1)} %feat.1, f32[1,512]{1,0:T(1,128)} %bitcast.12, f32[1,512]{1,0:T(1,128)} %bitcast.13, bf16[3456,256]{1,0:T(8,128)(2,1)} %bitcast.9, f32[1,256]{1,0:T(1,128)} %bitcast.14, bf16[128,256]{1,0:T(8,128)(2,1)} %bitcast.11, f32[1,256]{1,0:T(1,128)} %bitcast.15, ...), custom_call_target="tpu_custom_call" | custom-call | flops 2088763392 | bytes 4194304 | tf_op jit(solution)/shard_map/residual_block/pallas_call | solution.py:688
  37.0 1.5 %copy.12 = bf16[2,6,16,256]{3,2,1,0:T(8,128)(2,1)} copy(bf16[2,6,16,256]{3,2,1,0:T(8,128)(2,1)} %residual_block.1) | data formatting | bytes 196608

commit v5 on v4

--- a/solution.py
+++ b/solution.py
@@ -177,10 +177,10 @@
     feat, gain1_hbm, shift1_hbm, w1, bias1_hbm, wskip, gain2_hbm, shift2_hbm, w2, bias2_hbm,
     out,
     gain1, shift1, bias1, gain2, shift2, bias2, featv, xall, w1v, wsv, wcat, xp1, xp2,
-    acc, part1, send1, recv1, sum1, send1b, recv1b, stat0, other0, statg, stat2,
+    acc, part1, send1, recv1, sum1, send1b, recv1b, stat0, stat2,
     mids, midbf, prevbf, scut, part2, send2, recv2, sum2, send2b, recv2b,
     w_sem, p_sem, own_sem, fs_sem, fr_sem, fps_sem, fpr_sem,
-    s1s_sem, s1r_sem, sgs_sem, sgr_sem, s2s_sem, s2r_sem,
+    s1s_sem, s1r_sem, s2s_sem, s2r_sem,
     r1s_sem, r1r_sem, r1bs_sem, r1br_sem, r2s_sem, r2r_sem, r2bs_sem, r2br_sem,
     ps_sem, pr_sem,
 ):
@@ -206,10 +206,7 @@
     def slab(delta):
         return lax.rem(t + delta, slabs)
 
-    bits = [1 << k for k in range(slabs.bit_length() - 1)]
-
-    def across(bit):
-        return t + bit - 2 * bit * lax.rem(lax.div(t, bit), 2)
+    everyone = [(dt, di) for dt in range(slabs) for di in range(n) if dt or di]
 
     loads = [
         pltpu.make_async_copy(w1, w1v, w_sem.at[0]),
@@ -249,18 +246,10 @@
     own.start()
 
     barrier = pltpu.get_barrier_semaphore()
-    for delta in range(1, n):
-        pl.semaphore_signal(barrier, inc=1, device_id=ident(t, member(delta)), device_id_type=MESH)
-    for bit in bits:
-        pl.semaphore_signal(barrier, inc=1, device_id=ident(across(bit), me), device_id_type=MESH)
-
-    @pl.when(t > 0)
-    def _():
-        for delta in range(n):
-            pl.semaphore_signal(
-                barrier, inc=1, device_id=ident(t - 1, member(delta)), device_id_type=MESH
-            )
-
+    for dt, di in everyone:
+        pl.semaphore_signal(
+            barrier, inc=1, device_id=ident(slab(dt), member(di)), device_id_type=MESH
+        )
     for load in params + loads:
         load.start()
     blank = jnp.zeros((9, per2, wcat.shape[4]), wcat.dtype)
@@ -278,9 +267,10 @@
         at = slice(d * LANES, (d + 1) * LANES)
         tile = jnp.where(row8 == d, lane_mean[:, at], tile)
         tile = jnp.where(row8 == n + d, lane_spread[:, at], tile)
-    stat0[0] = tile
-
-    pl.semaphore_wait(barrier, jnp.where(t < slabs - 1, 2 * n - 1, n - 1) + len(bits))
+    here = t * n + me
+    stat0[here] = tile
+
+    pl.semaphore_wait(barrier, len(everyone))
 
     def stat_copy(buf, source, target, ssem, rsem):
         return pltpu.make_async_remote_copy(
@@ -289,33 +279,15 @@
             device_id=ident(target, me), device_id_type=MESH,
         )
 
-    def share_copy(source, target):
+    def tile_copy(source, t_to, to):
         return pltpu.make_async_remote_copy(
-            src_ref=statg.at[source], dst_ref=statg.at[source],
-            send_sem=sgs_sem.at[target], recv_sem=sgr_sem.at[source],
-            device_id=ident(t, target), device_id_type=MESH,
-        )
-
-    def swap_copy(k):
-        return pltpu.make_async_remote_copy(
-            src_ref=stat0.at[k], dst_ref=other0.at[k],
-            send_sem=s1s_sem.at[k], recv_sem=s1r_sem.at[k],
-            device_id=ident(across(bits[k]), me), device_id_type=MESH,
-        )
-
-    def swap(k):
-        swap_copy(k).wait_recv()
-        mine, theirs = stat0[k], other0[k]
-        off = (mine - theirs) ** 2 * (spots * bits[k] * 0.5)
-        total = mine + theirs
-        joined = jnp.where(row8 < n, 0.5 * total, total + pltpu.roll(off, n, 0))
-        if k + 1 < len(bits):
-            stat0[k + 1] = joined
-            swap_copy(k + 1).start()
-        else:
-            statg[me] = joined
-
-    swap_copy(0).start()
+            src_ref=stat0.at[source], dst_ref=stat0.at[source],
+            send_sem=s1s_sem.at[t_to * n + to], recv_sem=s1r_sem.at[source],
+            device_id=ident(t_to, to), device_id_type=MESH,
+        )
+
+    for dt, di in reversed(everyone):
+        tile_copy(here, slab(dt), member(di)).start()
 
     def feat_copy(source, target):
         return pltpu.make_async_remote_copy(
@@ -333,8 +305,6 @@
 
     for delta in reversed(range(1, n)):
         feat_copy(me, member(delta)).start()
-
-    swap(0)
 
     @pl.when(t < slabs - 1)
     def _():
@@ -370,11 +340,6 @@
     g1, b1 = own_full(gain1), own_full(shift1)
     g2, b2, c1 = own_twice(gain2), own_twice(shift2), own_twice(bias1)
 
-    for k in range(1, len(bits)):
-        swap(k)
-    for delta in reversed(range(1, n)):
-        share_copy(me, member(delta)).start()
-
     own.wait()
     for delta in range(1, n):
         feat_copy(member(delta), me).wait_recv()
@@ -383,13 +348,13 @@
         x = xall[2 + f].reshape(area, LANES)
         scut[f] = jnp.dot(x, wsv[...], preferred_element_type=jnp.float32)
 
-    for delta in range(1, n):
-        share_copy(member(delta), me).wait_recv()
-    stats = statg[...]
+    for dt, di in everyone:
+        tile_copy(slab(dt) * n + member(di), t, me).wait_recv()
+    stats = stat0[...]
     pick = lax.broadcasted_iota(jnp.int32, stats.shape, 1)
     means = jnp.sum(jnp.where(pick == me, stats, 0.0), axis=1, keepdims=True)
     spreads = jnp.sum(jnp.where(pick == n + me, stats, 0.0), axis=1, keepdims=True)
-    mean, inv = group_stats(means, spreads, same1, size1, spots * slabs)
+    mean, inv = group_stats(means, spreads, same1, size1, spots)
     scale = inv * g1
 
     def normalise(f):
@@ -509,9 +474,8 @@
 
     for delta in range(1, n):
         feat_copy(me, member(delta)).wait_send()
-        share_copy(me, member(delta)).wait_send()
-    for k in range(len(bits)):
-        swap_copy(k).wait_send()
+    for dt, di in everyone:
+        tile_copy(here, slab(dt), member(di)).wait_send()
 
     @pl.when(t < slabs - 1)
     def _():
@@ -631,7 +595,7 @@
     height, width = nrow * rows, ncol * cols
     area = height * width
     fits = frames == 2 and per1 == LANES and 2 * per2 == LANES and cols % 16 == 0
-    fits = fits and n == 4 and slabs & (slabs - 1) == 0 and width & (width - 1) == 0 and GROUPS % n == 0 and height % 2 == 0
+    fits = fits and n == 4 and width & (width - 1) == 0 and GROUPS % n == 0 and height % 2 == 0
     if not fits:
         return per_device_gathered(
             features, gn1_gain, gn1_bias, conv1_weight, conv1_bias, skip_weight,
@@ -661,9 +625,7 @@
         vmem((2, nrow, half, LANES), f32),
         vmem((2, nrow, half, LANES), bf16),
         vmem((2, nrow, half, LANES), bf16),
-        vmem((slabs, 2 * n, LANES), f32),
-        vmem((slabs, 2 * n, LANES), f32),
-        vmem((n, 2 * n, LANES), f32),
+        vmem((slabs * n, 2 * n, LANES), f32),
         vmem((slabs, 8, LANES), f32),
         vmem((2, 2, half, LANES), f32),
         vmem((2, half, LANES), bf16),
@@ -676,7 +638,7 @@
         vmem((2, nrow, rows, cols, chans_out), bf16),
         vmem((2, nrow, rows, cols, chans_out), bf16),
         dma((8,)), dma((6,)), dma((2,)), dma((n,)), dma((n,)), dma((n,)), dma((n,)),
-        dma((slabs,)), dma((slabs,)), dma((n,)), dma((n,)), dma((slabs,)), dma((slabs,)),
+        dma((slabs * n,)), dma((slabs * n,)), dma((slabs,)), dma((slabs,)),
         dma((2, ncol)), dma((2, ncol)), dma((2, nrow)), dma((2, nrow)),
         dma((2, ncol)), dma((2, ncol)), dma((2, nrow)), dma((2, nrow)),
         dma((2,)), dma((2,)),

time: 38.6 us -> 36.4 us (0.943)
  Pallas kernels: 37 us -> 34.8 us
    pallas_call x1, Pallas kernels: 37 us -> 34.8 us  [per_device(): pl.pallas_call(functools.partial(block_kernel, sizes), out_shape=jax.Shap...]
where the time goes in v5:
time: 36.4 us; the launch traced here: 36.3 us
  Pallas kernels  34.8 us (96%)
  local copies, waits for them, and re-layouts  1.54 us (4%)
    pallas_call x1, Pallas kernels, per_device(): pl.pallas_call(functools.partial(block_kernel, sizes), out_shape=jax.Shap...  34.8 us
    unnamed x1, local copies, waits for them, and re-layouts  1.54 us

profile of v5, /device:TPU:0, one launch (start us, length us, event | category | flops | bytes accessed | tf_op | source)
XLA Modules:
  0.0 36.3 jit_solution(4164639089211248457)
XLA Ops:
  0.0 34.8 %residual_block.1 = bf16[2,6,16,256]{3,2,1,0:T(8,128)(2,1)} custom-call(bf16[2,6,16,512]{3,2,1,0:T(8,128)(2,1)} %feat.1, f32[1,512]{1,0:T(1,128)} %bitcast.12, f32[1,512]{1,0:T(1,128)} %bitcast.13, bf16[3456,256]{1,0:T(8,128)(2,1)} %bitcast.9, f32[1,256]{1,0:T(1,128)} %bitcast.14, bf16[128,256]{1,0:T(8,128)(2,1)} %bitcast.11, f32[1,256]{1,0:T(1,128)} %bitcast.15, ...), custom_call_target="tpu_custom_call" | custom-call | flops 2088763392 | bytes 4194304 | tf_op jit(solution)/shard_map/residual_block/pallas_call | solution.py:650
  34.8 1.5 %copy.12 = bf16[2,6,16,256]{3,2,1,0:T(8,128)(2,1)} copy(bf16[2,6,16,256]{3,2,1,0:T(8,128)(2,1)} %residual_block.1) | data formatting | bytes 196608

commit v6 on v3

--- a/solution.py
+++ b/solution.py
@@ -147,21 +147,25 @@
     return jnp.where(row == 0, mean, jnp.where(row == 1, spread, 0.0))
 
 
+def group_sums(x, same):
+    high = x.astype(jnp.bfloat16).astype(jnp.float32)
+    rest = x - high
+    middle = rest.astype(jnp.bfloat16).astype(jnp.float32)
+    row = lax.broadcasted_iota(jnp.int32, (16, LANES), 0)
+    parts = jnp.where(row == 0, high, jnp.where(row == 1, middle, rest - middle))
+    parts = jnp.where(row < 3, parts, 0.0).astype(jnp.bfloat16)
+    sums = jnp.dot(parts, same, preferred_element_type=jnp.float32)
+    return jnp.sum(sums, axis=0, keepdims=True)
+
+
 def group_stats(means, spreads, same, lanes, count):
     parts = means.shape[0]
     mean = jnp.sum(means, axis=0) * (1.0 / parts)
     spread = jnp.sum(spreads, axis=0) + count * jnp.sum((means - mean[None]) ** 2, axis=0)
-    mean = jnp.broadcast_to(mean, (8, LANES))
-    group_mean = (
-        jnp.dot(mean, same, precision=lax.Precision.HIGHEST, preferred_element_type=jnp.float32)
-        * (1.0 / lanes)
-    )
+    group_mean = group_sums(mean, same) * (1.0 / lanes)
     spread = spread + (count * parts) * (mean - group_mean) ** 2
-    total = jnp.dot(
-        spread, same, precision=lax.Precision.HIGHEST, preferred_element_type=jnp.float32
-    )
-    inv = lax.rsqrt(total * (1.0 / (count * parts * lanes)) + 1e-6)
-    return group_mean[0:1], inv[0:1]
+    total = group_sums(spread, same)
+    return group_mean, lax.rsqrt(total * (1.0 / (count * parts * lanes)) + 1e-6)
 
 
 def side_shifts(h, cols):
@@ -308,12 +312,17 @@
             device_id=ident(to, target), device_id_type=MESH,
         )
 
+    @pl.when(t < slabs - 1)
+    def _():
+        for delta in range(ncol):
+            feat_next(me, member(delta), t + 1).start()
+
     for delta in reversed(range(1, n)):
         feat_copy(me, member(delta)).start()
 
     @pl.when(t < slabs - 1)
     def _():
-        for delta in reversed(range(n)):
+        for delta in range(ncol, n):
             feat_next(me, member(delta), t + 1).start()
 
     lane = lane_of((8, LANES))
@@ -321,8 +330,8 @@
     lane_to = lane_of((LANES, LANES))
     size1 = per1 // (GROUPS // n)
     size2 = per2 // (GROUPS // n)
-    same1 = (lane_in // size1 == lane_to // size1).astype(jnp.float32)
-    same2 = ((lane_in % per2) // size2 == (lane_to % per2) // size2).astype(jnp.float32)
+    same1 = (lane_in // size1 == lane_to // size1).astype(jnp.bfloat16)
+    same2 = ((lane_in % per2) // size2 == (lane_to % per2) // size2).astype(jnp.bfloat16)
 
     def own_full(ref):
         result = ref[0:1, 0:LANES]
@@ -453,6 +462,18 @@
             row_copy(send_b, recv_b, other, r, s, ssem_b, rsem_b).wait_recv()
             result = result + recv_b[s, other].astype(jnp.float32)
         return result
+
+    def sent_to_cores(stage):
+        send, recv, ssem, rsem = stage
+        for s in range(2):
+            for core in cores:
+                core_copy(send, recv, c, core, s, ssem, rsem).wait_send()
+
+    def sent_to_rows(stage):
+        send, recv, ssem, rsem = stage
+        for s in range(2):
+            for other in others:
+                row_copy(send, recv, r, other, s, ssem, rsem).wait_send()
 
     first = (send1, recv1, r1s_sem, r1r_sem)
     first_b = (send1b, recv1b, r1bs_sem, r1br_sem)
@@ -475,6 +496,17 @@
     for s in range(2):
         to_rows(first, part1, sum1, first_b, s)
 
+    for delta in range(1, n):
+        feat_copy(me, member(delta)).wait_send()
+        share_copy(me, member(delta)).wait_send()
+    for delta in range(1, slabs):
+        stat_copy(stat0, t, slab(delta), s1s_sem, s1r_sem).wait_send()
+
+    @pl.when(t < slabs - 1)
+    def _():
+        for delta in range(n):
+            feat_next(me, member(delta), t + 1).wait_send()
+
     def mid_copy(to, s):
         return pltpu.make_async_remote_copy(
             src_ref=midbf.at[s], dst_ref=prevbf.at[s],
@@ -501,6 +533,8 @@
 
     for delta in range(1, slabs):
         stat_copy(stat2, slab(delta), t, s2s_sem, s2r_sem).wait_recv()
+    sent_to_cores(first)
+    sent_to_rows(first_b)
     stats = stat2[...]
     mean, inv = group_stats(stats[:, 0:1], stats[:, 1:2], same2, 2 * size2, float(area))
     scale = inv * g2
@@ -550,31 +584,20 @@
         to_cores(second, f)
     for f in range(2):
         to_rows(second, part2, sum2, second_b, f)
+    for delta in range(1, slabs):
+        stat_copy(stat2, t, slab(delta), s2s_sem, s2r_sem).wait_send()
+
+    @pl.when(t < slabs - 1)
+    def _():
+        for s in range(2):
+            mid_copy(t + 1, s).wait_send()
+
+    sent_to_cores(second)
     last = bias2[...].reshape(1, 1, -1)
     for f in range(2):
         out[f] = (from_rows(sum2, second_b, f) + last).astype(out.dtype)
 
-    for delta in range(1, n):
-        target = member(delta)
-        feat_copy(me, target).wait_send()
-        share_copy(me, target).wait_send()
-    for s in range(2):
-        for send, recv, ssem, rsem in (first, second):
-            for core in cores:
-                core_copy(send, recv, c, core, s, ssem, rsem).wait_send()
-        for send, recv, ssem, rsem in (first_b, second_b):
-            for other in others:
-                row_copy(send, recv, r, other, s, ssem, rsem).wait_send()
-    for delta in range(1, slabs):
-        stat_copy(stat0, t, slab(delta), s1s_sem, s1r_sem).wait_send()
-        stat_copy(stat2, t, slab(delta), s2s_sem, s2r_sem).wait_send()
-
-    @pl.when(t < slabs - 1)
-    def _():
-        for delta in range(n):
-            feat_next(me, member(delta), t + 1).wait_send()
-        for s in range(2):
-            mid_copy(t + 1, s).wait_send()
+    sent_to_rows(second_b)
 
 
 def per_device(
@@ -650,20 +673,7 @@
     inside = pl.BlockSpec(memory_space=pltpu.VMEM)
     sizes = (slabs, nrow, ncol, rows, cols, per1, per2)
     flops = 2 * 2 * area * chans_out * (28 * per1 + 27 * per2)
-    return pl.pallas_call(
-        functools.partial(block_kernel, sizes),
-        out_shape=jax.ShapeDtypeStruct((frames, rows, cols, chans_out), bf16),
-        in_specs=[stays] * 10,
-        out_specs=inside,
-        scratch_shapes=scratch,
-        compiler_params=pltpu.CompilerParams(
-            collective_id=0, has_side_effects=True, vmem_limit_bytes=64 * 1024 * 1024
-        ),
-        cost_estimate=pl.CostEstimate(
-            flops=flops, bytes_accessed=4 * 1024 * 1024, transcendentals=6 * area * LANES
-        ),
-        name="residual_block",
-    )(
+    operands = (
         features,
         gn1_gain.reshape(1, -1),
         gn1_bias.reshape(1, -1),
@@ -675,6 +685,20 @@
         conv2_weight.reshape(3, 9, per2, chans_out),
         conv2_bias.reshape(1, -1),
     )
+    return pl.pallas_call(
+        functools.partial(block_kernel, sizes),
+        out_shape=jax.ShapeDtypeStruct((frames, rows, cols, chans_out), bf16),
+        in_specs=[stays] * 10,
+        out_specs=inside,
+        scratch_shapes=scratch,
+        compiler_params=pltpu.CompilerParams(
+            collective_id=0, has_side_effects=True, vmem_limit_bytes=48 * 1024 * 1024
+        ),
+        cost_estimate=pl.CostEstimate(
+            flops=flops, bytes_accessed=4 * 1024 * 1024, transcendentals=6 * area * LANES
+        ),
+        name="residual_block",
+    )(*(pltpu.with_memory_space_constraint(x, pltpu.HBM) for x in operands))
 
 
 def solution(mesh):

time: 36 us -> 34.1 us (0.947)
  Pallas kernels: 34.3 us -> 33.3 us
  local copies, waits for them, and re-layouts: 1.54 us -> 0.64 us
    pallas_call x1, Pallas kernels: 34.3 us -> 33.3 us  [per_device(): pl.pallas_call(functools.partial(block_kernel, sizes), out_shape=jax.Shap...]
    unnamed x1, local copies, waits for them, and re-layouts: 1.54 us -> 0.64 us
where the time goes in v6:
time: 34.1 us; the launch traced here: 34 us
  Pallas kernels  33.3 us (98%)
  local copies, waits for them, and re-layouts  0.64 us (2%)
    pallas_call x1, Pallas kernels, per_device(): pl.pallas_call(functools.partial(block_kernel, sizes), out_shape=jax.Shap...  33.3 us

profile of v6, /device:TPU:0, one launch (start us, length us, event | category | flops | bytes accessed | tf_op | source)
XLA Modules:
  0.0 34.0 jit_solution(6145445075798596882)
XLA Ops:
  0.0 33.3 %residual_block.1 = bf16[2,6,16,256]{3,2,1,0:T(8,128)(2,1)S(1)} custom-call(bf16[2,6,16,512]{3,2,1,0:T(8,128)(2,1)} %feat.1, f32[1,512]{1,0:T(1,128)} %bitcast.12, f32[1,512]{1,0:T(1,128)} %bitcast.13, bf16[3456,256]{1,0:T(8,128)(2,1)} %bitcast.9, f32[1,256]{1,0:T(1,128)} %bitcast.14, bf16[128,256]{1,0:T(8,128)(2,1)} %bitcast.11, f32[1,256]{1,0:T(1,128)} %bitcast.15, ...), custom_call_target="tpu_custom_call" | custom-call | flops 2088763392 | bytes 4194304 | tf_op jit(solution)/shard_map/residual_block/pallas_call | solution.py:688
  33.3 0.6 %copy.12 = bf16[2,6,16,256]{3,2,1,0:T(8,128)(2,1)} copy(bf16[2,6,16,256]{3,2,1,0:T(8,128)(2,1)S(1)} %residual_block.1) | data formatting | bytes 196608

commit v7 on v6

--- a/solution.py
+++ b/solution.py
@@ -210,6 +210,14 @@
     def slab(delta):
         return lax.rem(t + delta, slabs)
 
+    q = slabs // 2
+    side = lax.div(t, q)
+    spot = lax.rem(t, q)
+    far = slab(q)
+
+    def near(delta):
+        return side * q + lax.rem(spot + delta, q)
+
     loads = [
         pltpu.make_async_copy(w1, w1v, w_sem.at[0]),
         pltpu.make_async_copy(wskip, wsv, w_sem.at[1]),
@@ -250,12 +258,14 @@
     barrier = pltpu.get_barrier_semaphore()
     for delta in range(1, n):
         pl.semaphore_signal(barrier, inc=1, device_id=ident(t, member(delta)), device_id_type=MESH)
-    for delta in range(1, slabs):
-        pl.semaphore_signal(barrier, inc=1, device_id=ident(slab(delta), me), device_id_type=MESH)
+    for delta in range(1, q):
+        pl.semaphore_signal(barrier, inc=1, device_id=ident(near(delta), me), device_id_type=MESH)
+    for delta in range(n):
+        pl.semaphore_signal(barrier, inc=1, device_id=ident(far, member(delta)), device_id_type=MESH)
 
     @pl.when(t > 0)
     def _():
-        for delta in range(1, n):
+        for delta in range(n):
             pl.semaphore_signal(
                 barrier, inc=1, device_id=ident(t - 1, member(delta)), device_id_type=MESH
             )
@@ -277,9 +287,9 @@
         at = slice(d * LANES, (d + 1) * LANES)
         tile = jnp.where(row8 == d, lane_mean[:, at], tile)
         tile = jnp.where(row8 == n + d, lane_spread[:, at], tile)
-    stat0[t] = tile
-
-    pl.semaphore_wait(barrier, jnp.where(t < slabs - 1, 2 * (n - 1), n - 1) + slabs - 1)
+    stat0[spot] = tile
+
+    pl.semaphore_wait(barrier, jnp.where(t < slabs - 1, n, 0) + 2 * n + q - 2)
 
     def stat_copy(buf, source, target, ssem, rsem):
         return pltpu.make_async_remote_copy(
@@ -288,15 +298,26 @@
             device_id=ident(target, me), device_id_type=MESH,
         )
 
-    def share_copy(source, target):
+    def near_copy(source, target):
         return pltpu.make_async_remote_copy(
-            src_ref=statg.at[source], dst_ref=statg.at[source],
-            send_sem=sgs_sem.at[target], recv_sem=sgr_sem.at[source],
-            device_id=ident(t, target), device_id_type=MESH,
-        )
-
-    for delta in reversed(range(1, slabs)):
-        stat_copy(stat0, t, slab(delta), s1s_sem, s1r_sem).start()
+            src_ref=stat0.at[lax.rem(source, q)], dst_ref=stat0.at[lax.rem(source, q)],
+            send_sem=s1s_sem.at[lax.rem(target, q)], recv_sem=s1r_sem.at[lax.rem(source, q)],
+            device_id=ident(target, me), device_id_type=MESH,
+        )
+
+    def share_copy(t_from, source, t_to, target):
+        slot = lax.div(t_from, q) * n + source
+        return pltpu.make_async_remote_copy(
+            src_ref=statg.at[slot], dst_ref=statg.at[slot],
+            send_sem=sgs_sem.at[lax.div(t_to, q) * n + target], recv_sem=sgr_sem.at[slot],
+            device_id=ident(t_to, target), device_id_type=MESH,
+        )
+
+    sharers = [(far, delta) for delta in reversed(range(n))]
+    sharers += [(t, delta) for delta in reversed(range(1, n))]
+
+    for delta in reversed(range(1, q)):
+        near_copy(t, near(delta)).start()
 
     def feat_copy(source, target):
         return pltpu.make_async_remote_copy(
@@ -319,6 +340,16 @@
 
     for delta in reversed(range(1, n)):
         feat_copy(me, member(delta)).start()
+
+    for delta in range(1, q):
+        near_copy(near(delta), t).wait_recv()
+    stats = stat0[...]
+    total = jnp.sum(stats, axis=0)
+    mean = total * (1.0 / q)
+    off = spots * jnp.sum((stats - mean[None]) ** 2, axis=0)
+    statg[side * n + me] = jnp.where(row8 < n, mean, total + pltpu.roll(off, n, 0))
+    for slab_to, delta in sharers:
+        share_copy(t, me, slab_to, member(delta)).start()
 
     @pl.when(t < slabs - 1)
     def _():
@@ -354,16 +385,6 @@
     g1, b1 = own_full(gain1), own_full(shift1)
     g2, b2, c1 = own_twice(gain2), own_twice(shift2), own_twice(bias1)
 
-    for delta in range(1, slabs):
-        stat_copy(stat0, slab(delta), t, s1s_sem, s1r_sem).wait_recv()
-    stats = stat0[...]
-    total = jnp.sum(stats, axis=0)
-    mean = total * (1.0 / slabs)
-    off = spots * jnp.sum((stats - mean[None]) ** 2, axis=0)
-    statg[me] = jnp.where(row8 < n, mean, total + pltpu.roll(off, n, 0))
-    for delta in reversed(range(1, n)):
-        share_copy(me, member(delta)).start()
-
     own.wait()
     for delta in range(1, n):
         feat_copy(member(delta), me).wait_recv()
@@ -372,13 +393,13 @@
         x = xall[2 + f].reshape(area, LANES)
         scut[f] = jnp.dot(x, wsv[...], preferred_element_type=jnp.float32)
 
-    for delta in range(1, n):
-        share_copy(member(delta), me).wait_recv()
+    for slab_from, delta in sharers:
+        share_copy(slab_from, member(delta), t, me).wait_recv()
     stats = statg[...]
     pick = lax.broadcasted_iota(jnp.int32, stats.shape, 1)
     means = jnp.sum(jnp.where(pick == me, stats, 0.0), axis=1, keepdims=True)
     spreads = jnp.sum(jnp.where(pick == n + me, stats, 0.0), axis=1, keepdims=True)
-    mean, inv = group_stats(means, spreads, same1, size1, spots * slabs)
+    mean, inv = group_stats(means, spreads, same1, size1, spots * q)
     scale = inv * g1
 
     def normalise(f):
@@ -498,9 +519,10 @@
 
     for delta in range(1, n):
         feat_copy(me, member(delta)).wait_send()
-        share_copy(me, member(delta)).wait_send()
-    for delta in range(1, slabs):
-        stat_copy(stat0, t, slab(delta), s1s_sem, s1r_sem).wait_send()
+    for slab_to, delta in sharers:
+        share_copy(t, me, slab_to, member(delta)).wait_send()
+    for delta in range(1, q):
+        near_copy(t, near(delta)).wait_send()
 
     @pl.when(t < slabs - 1)
     def _():
@@ -620,7 +642,7 @@
     height, width = nrow * rows, ncol * cols
     area = height * width
     fits = frames == 2 and per1 == LANES and 2 * per2 == LANES and cols % 16 == 0
-    fits = fits and n == 4 and width & (width - 1) == 0 and GROUPS % n == 0 and height % 2 == 0
+    fits = fits and n == 4 and slabs % 2 == 0 and width & (width - 1) == 0 and GROUPS % n == 0 and height % 2 == 0
     if not fits:
         return per_device_gathered(
             features, gn1_gain, gn1_bias, conv1_weight, conv1_bias, skip_weight,
@@ -650,8 +672,8 @@
         vmem((2, nrow, half, LANES), f32),
         vmem((2, nrow, half, LANES), bf16),
         vmem((2, nrow, half, LANES), bf16),
-        vmem((slabs, 2 * n, LANES), f32),
-        vmem((n, 2 * n, LANES), f32),
+        vmem((slabs // 2, 2 * n, LANES), f32),
+        vmem((2 * n, 2 * n, LANES), f32),
         vmem((slabs, 8, LANES), f32),
         vmem((2, 2, half, LANES), f32),
         vmem((2, half, LANES), bf16),
@@ -664,7 +686,7 @@
         vmem((2, nrow, rows, cols, chans_out), bf16),
         vmem((2, nrow, rows, cols, chans_out), bf16),
         dma((8,)), dma((6,)), dma((2,)), dma((n,)), dma((n,)), dma((n,)), dma((n,)),
-        dma((slabs,)), dma((slabs,)), dma((n,)), dma((n,)), dma((slabs,)), dma((slabs,)),
+        dma((slabs,)), dma((slabs,)), dma((2 * n,)), dma((2 * n,)), dma((slabs,)), dma((slabs,)),
         dma((2, ncol)), dma((2, ncol)), dma((2, nrow)), dma((2, nrow)),
         dma((2, ncol)), dma((2, ncol)), dma((2, nrow)), dma((2, nrow)),
         dma((2,)), dma((2,)),

time: 34.1 us -> 32.9 us (0.965)
  Pallas kernels: 33.3 us -> 32.1 us
    pallas_call x1, Pallas kernels: 33.3 us -> 32.1 us  [per_device(): pl.pallas_call(functools.partial(block_kernel, sizes), out_shape=jax.Shap...]
where the time goes in v7:
time: 32.9 us; the launch traced here: 32.8 us
  Pallas kernels  32.1 us (98%)
  local copies, waits for them, and re-layouts  0.64 us (2%)
    pallas_call x1, Pallas kernels, per_device(): pl.pallas_call(functools.partial(block_kernel, sizes), out_shape=jax.Shap...  32.1 us

profile of v7, /device:TPU:0, one launch (start us, length us, event | category | flops | bytes accessed | tf_op | source)
XLA Modules:
  0.0 32.8 jit_solution(4713187964970428945)
XLA Ops:
  0.0 32.1 %residual_block.1 = bf16[2,6,16,256]{3,2,1,0:T(8,128)(2,1)S(1)} custom-call(bf16[2,6,16,512]{3,2,1,0:T(8,128)(2,1)} %feat.1, f32[1,512]{1,0:T(1,128)} %bitcast.12, f32[1,512]{1,0:T(1,128)} %bitcast.13, bf16[3456,256]{1,0:T(8,128)(2,1)} %bitcast.9, f32[1,256]{1,0:T(1,128)} %bitcast.14, bf16[128,256]{1,0:T(8,128)(2,1)} %bitcast.11, f32[1,256]{1,0:T(1,128)} %bitcast.15, ...), custom_call_target="tpu_custom_call" | custom-call | flops 2088763392 | bytes 4194304 | tf_op jit(solution)/shard_map/residual_block/pallas_call | solution.py:710
  32.1 0.6 %copy.12 = bf16[2,6,16,256]{3,2,1,0:T(8,128)(2,1)} copy(bf16[2,6,16,256]{3,2,1,0:T(8,128)(2,1)S(1)} %residual_block.1) | data formatting | bytes 196608

commit v8 on v7

--- a/solution.py
+++ b/solution.py
@@ -252,14 +252,8 @@
 
     whole = pltpu.make_async_copy(feat, featv, own_sem.at[1])
     whole.start()
-    own = pltpu.make_async_copy(chunk(me), window(2, me), own_sem.at[0])
-    own.start()
 
     barrier = pltpu.get_barrier_semaphore()
-    for delta in range(1, n):
-        pl.semaphore_signal(barrier, inc=1, device_id=ident(t, member(delta)), device_id_type=MESH)
-    for delta in range(1, q):
-        pl.semaphore_signal(barrier, inc=1, device_id=ident(near(delta), me), device_id_type=MESH)
     for delta in range(n):
         pl.semaphore_signal(barrier, inc=1, device_id=ident(far, member(delta)), device_id_type=MESH)
 
@@ -270,8 +264,12 @@
                 barrier, inc=1, device_id=ident(t - 1, member(delta)), device_id_type=MESH
             )
 
-    for load in params + loads:
-        load.start()
+    for delta in range(1, q):
+        pl.semaphore_signal(barrier, inc=1, device_id=ident(near(delta), me), device_id_type=MESH)
+    for delta in range(1, n):
+        pl.semaphore_signal(barrier, inc=1, device_id=ident(t, member(delta)), device_id_type=MESH)
+    own = pltpu.make_async_copy(chunk(me), window(2, me), own_sem.at[0])
+    own.start()
     blank = jnp.zeros((9, per2, wcat.shape[4]), wcat.dtype)
     wcat[0, 1, :, per2:, :] = blank
     wcat[1, 0, :, :per2, :] = blank
@@ -340,6 +338,9 @@
 
     for delta in reversed(range(1, n)):
         feat_copy(me, member(delta)).start()
+
+    for load in params + loads:
+        load.start()
 
     for delta in range(1, q):
         near_copy(near(delta), t).wait_recv()

time: 32.9 us -> 32.9 us (level)
  no operation moved by 1% of the time
where the time goes in v8:
time: 32.9 us; the launch traced here: 32.8 us
  Pallas kernels  32.1 us (98%)
  local copies, waits for them, and re-layouts  0.64 us (2%)
    pallas_call x1, Pallas kernels, per_device(): pl.pallas_call(functools.partial(block_kernel, sizes), out_shape=jax.Shap...  32.1 us

profile of v8, /device:TPU:0, one launch (start us, length us, event | category | flops | bytes accessed | tf_op | source)
XLA Modules:
  0.0 32.8 jit_solution(8936039197447616312)
XLA Ops:
  0.0 32.1 %residual_block.1 = bf16[2,6,16,256]{3,2,1,0:T(8,128)(2,1)S(1)} custom-call(bf16[2,6,16,512]{3,2,1,0:T(8,128)(2,1)} %feat.1, f32[1,512]{1,0:T(1,128)} %bitcast.12, f32[1,512]{1,0:T(1,128)} %bitcast.13, bf16[3456,256]{1,0:T(8,128)(2,1)} %bitcast.9, f32[1,256]{1,0:T(1,128)} %bitcast.14, bf16[128,256]{1,0:T(8,128)(2,1)} %bitcast.11, f32[1,256]{1,0:T(1,128)} %bitcast.15, ...), custom_call_target="tpu_custom_call" | custom-call | flops 2088763392 | bytes 4194304 | tf_op jit(solution)/shard_map/residual_block/pallas_call | solution.py:711
  32.1 0.6 %copy.12 = bf16[2,6,16,256]{3,2,1,0:T(8,128)(2,1)} copy(bf16[2,6,16,256]{3,2,1,0:T(8,128)(2,1)S(1)} %residual_block.1) | data formatting | bytes 196608
